TPU v7x, 32 devices: a whole 2x2x4 slice. The times are simulated.
32 devices in a mesh: group: 2 (over x), row: 8 (over z, y), col: 2 (over core).
Axes of the slice: x: 2, y: 2, z: 4, core: 2. Of those that a mesh axis runs over, the one named last changes fastest.
Arguments:
- homolog_features: bfloat16 [1024, 3072], P(('group', 'row')), parts along dimension 0, may hold values from -6 to 6
- normalizer_factor: float32 [64], replicated, may hold values from 0.5 to 1.5
- normalizer_shift: float32 [64], replicated, may hold values from -3 to 3
- first_weights_table: bfloat16 [64, 32], replicated, may hold values from -0.75 to 0.75
- second_weights_table: bfloat16 [64, 32], replicated, may hold values from -0.75 to 0.75
- output_matrix: bfloat16 [1024, 128], replicated, may hold values from -1.796875 to 1.796875
- output_bias: float32 [128], replicated, may hold values from -6 to 6
- pair_update_cotangent: bfloat16 [1024, 512, 128], P(('group', 'row'), 'col'), parts along dimension 0, may hold values from -1.796875 to 1.796875
Outputs:
- pair_delta: bfloat16 [1024, 512, 128], P(('group', 'row'), 'col'), parts along dimension 0
- alignment_gradient: bfloat16 [1024, 3072], P(('group', 'row')), parts along dimension 0
There are 2 independent parts, one for each index of `group`. A program takes and returns all parts, laid end to end along the dimension named above; an argument that names none is the same for every part. Nothing has to cross between parts.
All inputs are finite; a program needn't handle non-finite values.
Results may differ from a plain program's by a relative error of at most 0.0064.
Values may be sent and summed in bfloat16 or wider, within the bound.
A program may use at most 192 MiB of HBM per device.

v0:
```python
import jax
import jax.numpy as jnp
from jax import lax
from jax.sharding import PartitionSpec as P

HOMOLOG_TOTAL = 48
FEATURE_WIDTH = 64
HIDDEN_WIDTH = 32
CZ = 128


def apply_layer_norm(homolog_features, normalizer_factor, normalizer_shift):
    entry_number = homolog_features.shape[0]
    quantity_tensor = homolog_features.astype(jnp.float32).reshape(
        entry_number, HOMOLOG_TOTAL, FEATURE_WIDTH
    )
    center = quantity_tensor - jnp.mean(quantity_tensor, axis=-1, keepdims=True)
    inverse_scale = lax.rsqrt(jnp.mean(center * center, axis=-1, keepdims=True) + 1e-05)
    standard_deviation = center * inverse_scale
    normalized_block = (standard_deviation * normalizer_factor + normalizer_shift).astype(
        jnp.bfloat16
    )
    return (normalized_block, standard_deviation, inverse_scale)


def project(normalized_block, weight):
    return jnp.einsum(
        "isc,ch->ihs", normalized_block, weight, preferred_element_type=jnp.float32
    ).astype(jnp.bfloat16)


def input_gradient(
    left_gradient,
    right_gradient,
    standard_deviation,
    inverse_scale,
    normalizer_factor,
    first_weights_table,
    second_weights_table,
):
    highest = lax.Precision.HIGHEST
    dnormed = jnp.einsum(
        "ihs,ch->isc", left_gradient, first_weights_table.astype(jnp.float32), precision=highest
    )
    dnormed = dnormed + jnp.einsum(
        "ihs,ch->isc", right_gradient, second_weights_table.astype(jnp.float32), precision=highest
    )
    scaled = dnormed * normalizer_factor
    result = inverse_scale * (
        scaled
        - jnp.mean(scaled, axis=-1, keepdims=True)
        - standard_deviation * jnp.mean(scaled * standard_deviation, axis=-1, keepdims=True)
    )
    return result.reshape(result.shape[0], -1).astype(jnp.bfloat16)


def pair_blocks(left_use, right_use, cot_use, output_matrix, output_bias):
    entry_number = left_use.shape[0]
    col_rows = right_use.shape[0]
    right_flat = right_use.reshape(col_rows * HIDDEN_WIDTH, HOMOLOG_TOTAL)
    weight_three = output_matrix.reshape(HIDDEN_WIDTH, HIDDEN_WIDTH, CZ)
    block_rows = 8
    block_count = entry_number // block_rows

    def advance(running, inputs):
        left_block, cot_block = inputs
        left_flat = left_block.reshape(block_rows * HIDDEN_WIDTH, HOMOLOG_TOTAL)
        outer = (
            lax.dot_general(
                left_flat, right_flat, (((1,), (1,)), ((), ())), preferred_element_type=jnp.float32
            )
            / HOMOLOG_TOTAL
        )
        outer = outer.astype(jnp.bfloat16).reshape(block_rows, HIDDEN_WIDTH, col_rows, HIDDEN_WIDTH)
        update = (
            jnp.einsum("iajb,abk->ijk", outer, weight_three, preferred_element_type=jnp.float32)
            + output_bias
        )
        update = update.astype(jnp.bfloat16)
        grad_outer = jnp.einsum(
            "ijk,abk->iajb", cot_block, weight_three, preferred_element_type=jnp.float32
        ).astype(jnp.bfloat16)
        grad_flat = grad_outer.reshape(block_rows * HIDDEN_WIDTH, col_rows * HIDDEN_WIDTH)
        left_part = (
            jnp.dot(grad_flat, right_flat, preferred_element_type=jnp.float32) / HOMOLOG_TOTAL
        )
        right_part = (
            lax.dot_general(
                grad_flat, left_flat, (((0,), (0,)), ((), ())), preferred_element_type=jnp.float32
            )
            / HOMOLOG_TOTAL
        )
        return (
            running + right_part,
            (update, left_part.reshape(block_rows, HIDDEN_WIDTH, HOMOLOG_TOTAL)),
        )

    zero_sums = jnp.zeros((col_rows * HIDDEN_WIDTH, HOMOLOG_TOTAL), jnp.float32)
    right_sum, (updates, left_parts) = lax.scan(
        advance,
        zero_sums,
        (
            left_use.reshape(block_count, block_rows, HIDDEN_WIDTH, HOMOLOG_TOTAL),
            cot_use.reshape(block_count, block_rows, col_rows, CZ),
        ),
    )
    return (
        updates.reshape(entry_number, col_rows, CZ),
        left_parts.reshape(entry_number, HIDDEN_WIDTH, HOMOLOG_TOTAL),
        right_sum.reshape(col_rows, HIDDEN_WIDTH, HOMOLOG_TOTAL),
    )


def shards(
    homolog_features,
    normalizer_factor,
    normalizer_shift,
    first_weights_table,
    second_weights_table,
    output_matrix,
    output_bias,
    pair_update_cotangent,
):
    normalized_block, standard_deviation, inverse_scale = apply_layer_norm(
        homolog_features, normalizer_factor, normalizer_shift
    )
    left_proj = project(normalized_block, first_weights_table)
    right_proj = project(normalized_block, second_weights_table)
    right_all = lax.all_gather(right_proj, "row", axis=0, tiled=True)
    col_count = lax.axis_size("col")
    col_index = lax.axis_index("col")
    row_index = lax.axis_index("row")
    device_rows = homolog_features.shape[0]
    all_rows = right_all.shape[0]
    block_cols = all_rows // col_count
    right_use = lax.dynamic_slice_in_dim(right_all, col_index * block_cols, block_cols, 0)
    pair_delta, left_part, right_part = pair_blocks(
        left_proj, right_use, pair_update_cotangent, output_matrix, output_bias
    )
    left_gradient = lax.psum(left_part, "col")
    right_block = lax.psum(right_part, "row")
    offset = row_index * device_rows - col_index * block_cols
    inside = jnp.logical_and(offset >= 0, offset < block_cols).astype(jnp.float32)
    first_row = jnp.clip(offset, 0, block_cols - device_rows)
    own_part = lax.dynamic_slice_in_dim(right_block, first_row, device_rows, 0) * inside
    right_gradient = lax.psum(own_part, "col")
    alignment_gradient = input_gradient(
        left_gradient,
        right_gradient,
        standard_deviation,
        inverse_scale,
        normalizer_factor,
        first_weights_table,
        second_weights_table,
    )
    return (pair_delta, alignment_gradient)


def solution(mesh):
    in_specs = (
        P(("group", "row"), None),
        P(),
        P(),
        P(),
        P(),
        P(),
        P(),
        P(("group", "row"), "col", None),
    )
    out_specs = (P(("group", "row"), "col", None), P(("group", "row"), None))
    return jax.shard_map(shards, mesh=mesh, in_specs=in_specs, out_specs=out_specs, check_vma=False)
```

profile of v0, /device:TPU:0, one launch (start us, length us, event | category | flops | bytes accessed | tf_op | source)
XLA Modules:
  0.0 844.3 jit_solution(702310014841325239)
XLA Ops:
  13.7 74.9 %all-gather.2.cloned.1.call-done = bf16[512,32,48]{2,1,0:T(8,128)(2,1)} async-done(((bf16[64,32,48]{2,1,0:T(8,128)(2,1)}), bf16[512,32,48]{2,1,0:T(8,128)(2,1)}) %all-gather.2.cloned.1.call-update) | async-done | bytes 1572880 | tf_op jit(solution)/shard_map/all_gather | solution.py:129
  90.5 621.7 %while.15 = (s32[]{:T(128)}, f32[8192,48]{0,1:T(8,128)}, bf16[8,8,256,128]{3,2,1,0:T(8,128)(2,1)}, f32[8,8,32,48]{3,2,1,0:T(8,128)}, bf16[8,8,256,128]{3,2,1,0:T...) while((s32[]{:T(128)}, f32[8192,48]{0,1:T(8,128)}, ...), condition=%wide.region_3.4_spmd.clone, body=%wide.region_2.3_spmd.clone.sunk | while | flops 1685729280 | bytes 82217112 | solution.py:99
  95.0 14.4 %copy.57 = bf16[8,32,256,32]{3,2,1,0:T(8,128)(2,1)} copy(bf16[8,32,256,32]{2,3,1,0:T(8,128)(2,1)} %convert_bitcast_fusion.2) | data formatting | bytes 8388608 | tf_op jit(solution)/shard_map/while/body/eval_jaxpr/convert_element_type | solution.py:82
  109.4 21.7 %reshape.89 = bf16[256,8192]{1,0:T(8,128)(2,1)} reshape(bf16[8,32,256,32]{3,2,1,0:T(8,128)(2,1)} %copy.57) | data formatting | bytes 8388608 | tf_op jit(solution)/shard_map/while/body/eval_jaxpr/reshape | solution.py:83
  138.5 17.3 %reshape.90 = bf16[8,32,256,32]{3,2,1,0:T(8,128)(2,1)} reshape(bf16[256,8192]{1,0:T(8,128)(2,1)} %fusion.54) | data formatting | bytes 8388608 | tf_op jit(solution)/shard_map/while/body/eval_jaxpr/reshape | solution.py:74
  172.2 14.4 %copy.57 = bf16[8,32,256,32]{3,2,1,0:T(8,128)(2,1)} copy(bf16[8,32,256,32]{2,3,1,0:T(8,128)(2,1)} %convert_bitcast_fusion.2) | data formatting | bytes 8388608 | tf_op jit(solution)/shard_map/while/body/eval_jaxpr/convert_element_type | solution.py:82
  186.6 21.7 %reshape.89 = bf16[256,8192]{1,0:T(8,128)(2,1)} reshape(bf16[8,32,256,32]{3,2,1,0:T(8,128)(2,1)} %copy.57) | data formatting | bytes 8388608 | tf_op jit(solution)/shard_map/while/body/eval_jaxpr/reshape | solution.py:83
  216.2 17.3 %reshape.90 = bf16[8,32,256,32]{3,2,1,0:T(8,128)(2,1)} reshape(bf16[256,8192]{1,0:T(8,128)(2,1)} %fusion.54) | data formatting | bytes 8388608 | tf_op jit(solution)/shard_map/while/body/eval_jaxpr/reshape | solution.py:74
  250.0 14.4 %copy.57 = bf16[8,32,256,32]{3,2,1,0:T(8,128)(2,1)} copy(bf16[8,32,256,32]{2,3,1,0:T(8,128)(2,1)} %convert_bitcast_fusion.2) | data formatting | bytes 8388608 | tf_op jit(solution)/shard_map/while/body/eval_jaxpr/convert_element_type | solution.py:82
  264.4 21.7 %reshape.89 = bf16[256,8192]{1,0:T(8,128)(2,1)} reshape(bf16[8,32,256,32]{3,2,1,0:T(8,128)(2,1)} %copy.57) | data formatting | bytes 8388608 | tf_op jit(solution)/shard_map/while/body/eval_jaxpr/reshape | solution.py:83
  294.0 17.3 %reshape.90 = bf16[8,32,256,32]{3,2,1,0:T(8,128)(2,1)} reshape(bf16[256,8192]{1,0:T(8,128)(2,1)} %fusion.54) | data formatting | bytes 8388608 | tf_op jit(solution)/shard_map/while/body/eval_jaxpr/reshape | solution.py:74
  327.7 14.4 %copy.57 = bf16[8,32,256,32]{3,2,1,0:T(8,128)(2,1)} copy(bf16[8,32,256,32]{2,3,1,0:T(8,128)(2,1)} %convert_bitcast_fusion.2) | data formatting | bytes 8388608 | tf_op jit(solution)/shard_map/while/body/eval_jaxpr/convert_element_type | solution.py:82
  342.1 21.7 %reshape.89 = bf16[256,8192]{1,0:T(8,128)(2,1)} reshape(bf16[8,32,256,32]{3,2,1,0:T(8,128)(2,1)} %copy.57) | data formatting | bytes 8388608 | tf_op jit(solution)/shard_map/while/body/eval_jaxpr/reshape | solution.py:83
  371.7 17.3 %reshape.90 = bf16[8,32,256,32]{3,2,1,0:T(8,128)(2,1)} reshape(bf16[256,8192]{1,0:T(8,128)(2,1)} %fusion.54) | data formatting | bytes 8388608 | tf_op jit(solution)/shard_map/while/body/eval_jaxpr/reshape | solution.py:74
  419.9 21.7 %reshape.89 = bf16[256,8192]{1,0:T(8,128)(2,1)} reshape(bf16[8,32,256,32]{3,2,1,0:T(8,128)(2,1)} %copy.57) | data formatting | bytes 8388608 | tf_op jit(solution)/shard_map/while/body/eval_jaxpr/reshape | solution.py:83
  449.5 17.3 %reshape.90 = bf16[8,32,256,32]{3,2,1,0:T(8,128)(2,1)} reshape(bf16[256,8192]{1,0:T(8,128)(2,1)} %fusion.54) | data formatting | bytes 8388608 | tf_op jit(solution)/shard_map/while/body/eval_jaxpr/reshape | solution.py:74
  497.6 21.7 %reshape.89 = bf16[256,8192]{1,0:T(8,128)(2,1)} reshape(bf16[8,32,256,32]{3,2,1,0:T(8,128)(2,1)} %copy.57) | data formatting | bytes 8388608 | tf_op jit(solution)/shard_map/while/body/eval_jaxpr/reshape | solution.py:83
  527.2 17.3 %reshape.90 = bf16[8,32,256,32]{3,2,1,0:T(8,128)(2,1)} reshape(bf16[256,8192]{1,0:T(8,128)(2,1)} %fusion.54) | data formatting | bytes 8388608 | tf_op jit(solution)/shard_map/while/body/eval_jaxpr/reshape | solution.py:74
  575.4 21.7 %reshape.89 = bf16[256,8192]{1,0:T(8,128)(2,1)} reshape(bf16[8,32,256,32]{3,2,1,0:T(8,128)(2,1)} %copy.57) | data formatting | bytes 8388608 | tf_op jit(solution)/shard_map/while/body/eval_jaxpr/reshape | solution.py:83
  605.0 17.3 %reshape.90 = bf16[8,32,256,32]{3,2,1,0:T(8,128)(2,1)} reshape(bf16[256,8192]{1,0:T(8,128)(2,1)} %fusion.54) | data formatting | bytes 8388608 | tf_op jit(solution)/shard_map/while/body/eval_jaxpr/reshape | solution.py:74
  653.1 21.7 %reshape.89 = bf16[256,8192]{1,0:T(8,128)(2,1)} reshape(bf16[8,32,256,32]{3,2,1,0:T(8,128)(2,1)} %copy.57) | data formatting | bytes 8388608 | tf_op jit(solution)/shard_map/while/body/eval_jaxpr/reshape | solution.py:83
  682.7 17.3 %reshape.90 = bf16[8,32,256,32]{3,2,1,0:T(8,128)(2,1)} reshape(bf16[256,8192]{1,0:T(8,128)(2,1)} %fusion.54) | data formatting | bytes 8388608 | tf_op jit(solution)/shard_map/while/body/eval_jaxpr/reshape | solution.py:74
  725.9 84.3 %all-reduce.4.cloned.1.call-done = f32[256,32,48]{0,1,2:T(8,128)} async-done(((f32[256,32,48]{0,1,2:T(8,128)}), f32[256,32,48]{0,1,2:T(8,128)}) %all-reduce.4.cloned.1.call-update) | async-done | bytes 1572880 | tf_op jit(solution)/shard_map/psum | solution.py:141
  812.9 19.7 %all-reduce.6.cloned.1.call-done = (f32[64,32,48]{0,1,2:T(8,128)}, f32[64,32,48]{0,1,2:T(8,128)}) async-done(((f32[64,32,48]{0,1,2:T(8,128)}, f32[64,32,48]{0,1,2:T(8,128)}), (f32[64,32,48]{0,1,2:T(8,128)}, f32[64,32,48]{0,1,2:T(8,128)})) %all-reduce.6.cloned.1.call-update) | async-done | bytes 786448 | tf_op jit(solution)/shard_map/psum | solution.py:140
  (145 shorter events, 281.9 us)
Async XLA Ops:
  7.2 3.2 copy-start
  7.2 81.4 %all-gather.2.cloned.1.call-start = ((), (), s32[]{:S(2)}) async-start(), calls=%async_computation | async-start | bytes 4718592 | tf_op jit(solution)/shard_map/all_gather | solution.py:129
  8.5 1.2 copy-start.2
  8.8 1.4 copy-start.7
  10.3 2.1 copy-start.11
  12.3 798.0 %all-reduce.4.cloned.1.call-start = ((), (), s32[]{:S(2)}) async-start(), calls=%async_computation.1 | async-start | bytes 3145728 | tf_op jit(solution)/shard_map/psum | solution.py:141
  13.6 76.9 %copy-start.4 = (bf16[1024,128]{1,0:T(8,128)(2,1)S(1)}, bf16[1024,128]{1,0:T(8,128)(2,1)}, u32[]{:S(2)}) copy-start(bf16[1024,128]{1,0:T(8,128)(2,1)} %param.15) | copy-start | bytes 786436
  13.6 76.9 %copy-start.16 = (f32[128]{0:T(128)S(1)}, f32[128]{0:T(128)}, u32[]{:S(2)}) copy-start(f32[128]{0:T(128)} %param.16) | copy-start | bytes 1540
  155.7 10.1 %copy-start.1 = (bf16[256,8192]{1,0:T(8,128)(2,1)S(1)}, bf16[256,8192]{1,0:T(8,128)(2,1)}, u32[]{:S(2)}) copy-start(bf16[256,8192]{1,0:T(8,128)(2,1)} %reshape.89) | copy-start | bytes 12582916 | tf_op jit(solution)/shard_map/while
  233.5 10.1 %copy-start.1 = (bf16[256,8192]{1,0:T(8,128)(2,1)S(1)}, bf16[256,8192]{1,0:T(8,128)(2,1)}, u32[]{:S(2)}) copy-start(bf16[256,8192]{1,0:T(8,128)(2,1)} %reshape.89) | copy-start | bytes 12582916 | tf_op jit(solution)/shard_map/while
  311.2 10.1 %copy-start.1 = (bf16[256,8192]{1,0:T(8,128)(2,1)S(1)}, bf16[256,8192]{1,0:T(8,128)(2,1)}, u32[]{:S(2)}) copy-start(bf16[256,8192]{1,0:T(8,128)(2,1)} %reshape.89) | copy-start | bytes 12582916 | tf_op jit(solution)/shard_map/while
  389.0 10.1 %copy-start.1 = (bf16[256,8192]{1,0:T(8,128)(2,1)S(1)}, bf16[256,8192]{1,0:T(8,128)(2,1)}, u32[]{:S(2)}) copy-start(bf16[256,8192]{1,0:T(8,128)(2,1)} %reshape.89) | copy-start | bytes 12582916 | tf_op jit(solution)/shard_map/while
  466.7 10.1 %copy-start.1 = (bf16[256,8192]{1,0:T(8,128)(2,1)S(1)}, bf16[256,8192]{1,0:T(8,128)(2,1)}, u32[]{:S(2)}) copy-start(bf16[256,8192]{1,0:T(8,128)(2,1)} %reshape.89) | copy-start | bytes 12582916 | tf_op jit(solution)/shard_map/while
  544.5 10.1 %copy-start.1 = (bf16[256,8192]{1,0:T(8,128)(2,1)S(1)}, bf16[256,8192]{1,0:T(8,128)(2,1)}, u32[]{:S(2)}) copy-start(bf16[256,8192]{1,0:T(8,128)(2,1)} %reshape.89) | copy-start | bytes 12582916 | tf_op jit(solution)/shard_map/while
  622.3 10.1 %copy-start.1 = (bf16[256,8192]{1,0:T(8,128)(2,1)S(1)}, bf16[256,8192]{1,0:T(8,128)(2,1)}, u32[]{:S(2)}) copy-start(bf16[256,8192]{1,0:T(8,128)(2,1)} %reshape.89) | copy-start | bytes 12582916 | tf_op jit(solution)/shard_map/while
  700.0 10.1 %copy-start.1 = (bf16[256,8192]{1,0:T(8,128)(2,1)S(1)}, bf16[256,8192]{1,0:T(8,128)(2,1)}, u32[]{:S(2)}) copy-start(bf16[256,8192]{1,0:T(8,128)(2,1)} %reshape.89) | copy-start | bytes 12582916 | tf_op jit(solution)/shard_map/while
  722.9 1.2 copy-start.5
  723.0 109.6 %all-reduce.6.cloned.1.call-start = ((), (), s32[]{:S(2)}) async-start(), calls=%async_computation.2 | async-start | bytes 3145728 | tf_op jit(solution)/shard_map/psum | solution.py:140
  725.9 106.7 %copy-start.12 = (bf16[64,32]{0,1:T(8,128)(2,1)S(1)}, bf16[64,32]{0,1:T(8,128)(2,1)}, u32[]{:S(2)}) copy-start(bf16[64,32]{0,1:T(8,128)(2,1)} %param.13) | copy-start | bytes 12292
  812.8 21.8 %copy-start.8 = (f32[64,48]{0,1:T(8,128)S(1)}, f32[64,48]{0,1:T(8,128)}, u32[]{:S(2)}) copy-start(f32[64,48]{0,1:T(8,128)} %copy-done.7) | copy-start | bytes 36868
  812.8 21.8 %copy-start.10 = (f32[64,48]{0,1:T(8,128)S(1)}, f32[64,48]{0,1:T(8,128)}, u32[]{:S(2)}) copy-start(f32[64,48]{0,1:T(8,128)} %copy-done.9) | copy-start | bytes 36868
  812.9 21.8 %copy-start.3 = (f32[64,3072]{0,1:T(8,128)S(1)}, f32[64,3072]{0,1:T(8,128)}, u32[]{:S(2)}) copy-start(f32[64,3072]{0,1:T(8,128)} %copy-done.2) | copy-start | bytes 2359300
  812.9 21.8 %copy-start.14 = (f32[64]{0:T(128)S(1)}, f32[64]{0:T(128)}, u32[]{:S(2)}) copy-start(f32[64]{0:T(128)} %param.11) | copy-start | bytes 772
  832.6 2.1 copy-start.6
  (3 other events, 3.0 us)
Sparse Core Ops, SparseCore 0:
  12.4 76.0 all-gather.1
  723.1 87.1 all-reduce.3
  813.0 19.5 all-reduce.5
where the time goes:
time: 855 us; the launch traced here: 844 us
  local copies, waits for them, and re-layouts  454 us (53%)
  matrix products  193 us (23%)
  waiting for transfers between devices  179 us (21%)
  between operations  14 us (2%)
    reshape x8, local copies, waits for them, and re-layouts, advance(): grad_outer.reshape(block_rows * HIDDEN_WIDTH, col_rows * HIDDEN_WIDTH)  173 us
    reshape x8, local copies, waits for them, and re-layouts, advance(): outer.astype(jnp.bfloat16)  138 us
    convert_element_type x8, local copies, waits for them, and re-layouts, advance(): grad_outer = jnp.einsum('ijk,abk->iajb', cot_block, weight_three, preferr...  115 us
    psum x1, waiting for transfers between devices, shards(): right_block = lax.psum(right_part, 'row')  84.3 us
    dot_general x8, matrix products, advance(): jnp.einsum('iajb,abk->ijk', outer, weight_three, preferred_element_type=j...  80.7 us
    all_gather x1, waiting for transfers between devices, shards(): right_all = lax.all_gather(right_proj, 'row', axis=0, tiled=True)  74.9 us
    dot_general x8, matrix products, advance(): lax.dot_general(grad_flat, left_flat, (((0,), (0,)), ((), ())), preferred...  37.2 us
    dot_general x8, matrix products, advance(): jnp.einsum('ijk,abk->iajb', cot_block, weight_three, preferred_element_ty...  33.9 us
  transfers between devices with their start and end apart: 3, of which 3 were waited for; matrix products, arithmetic and copies ran while one was open for 0% of the time, Pallas kernels for 0%

commit v1 on v0

v1 whole, which is shorter than its diff:
```python
import functools

import jax
import jax.numpy as jnp
from jax import lax
from jax.experimental import pallas as pl
from jax.experimental.pallas import tpu as pltpu
from jax.sharding import PartitionSpec as P

SEQS = 48
CHANNELS = 64
HIDDEN = 32
BLOCK = 8


def pair_kernel(left_ref, right_ref, w_ref, wt_ref, bias_ref, cot_ref,
                out_ref, lg_ref, rg_ref, right_t, z, v, cots, total):
    step = pl.program_id(0)
    cols = right_ref.shape[0]
    cz = cot_ref.shape[2]
    scale = 1.0 / SEQS

    @pl.when(step == 0)
    def _():
        right_t[...] = right_ref[...].T
        total[...] = jnp.zeros_like(total)

    for i in range(BLOCK):
        cots[:, i * cz:(i + 1) * cz] = cot_ref[i]

    group = 4

    @pl.loop(0, HIDDEN // group)
    def _(g):
        lanes = pl.ds(pl.multiple_of(g * group * cz, group * cz), group * cz)
        part = jnp.dot(left_ref[...], w_ref[:, lanes],
                       preferred_element_type=jnp.float32).astype(jnp.bfloat16)
        for b in range(group):
            for i in range(BLOCK):
                rows = pl.ds(pl.multiple_of((g * group + b) * SEQS, 16), SEQS)
                z[rows, i * cz:(i + 1) * cz] = part[
                    i * SEQS:(i + 1) * SEQS, b * cz:(b + 1) * cz]

    @pl.loop(0, BLOCK // 2)
    def _(p):
        lanes = pl.ds(pl.multiple_of(p * 2 * cz, 2 * cz), 2 * cz)
        res = jnp.dot(right_ref[...], z[:, lanes],
                      preferred_element_type=jnp.float32) * scale
        for q in range(2):
            out_ref[2 * p + q] = (res[:, q * cz:(q + 1) * cz]
                                  + bias_ref[...]).astype(jnp.bfloat16)
        u = jnp.dot(right_t[...], cots[:, lanes],
                    preferred_element_type=jnp.float32).astype(jnp.bfloat16)
        for q in range(2):
            rows = pl.ds(pl.multiple_of((2 * p + q) * SEQS, 16), SEQS)
            for b in range(HIDDEN):
                v[rows, b * cz:(b + 1) * cz] = u[
                    b * SEQS:(b + 1) * SEQS, q * cz:(q + 1) * cz]

    lg_ref[...] = jnp.dot(v[...], wt_ref[...], preferred_element_type=jnp.float32) * scale
    total[...] += lax.dot_general(z[...], cots[...], (((1,), (1,)), ((), ())),
                                  preferred_element_type=jnp.float32)

    @pl.when(step == pl.num_programs(0) - 1)
    def _():
        rg_ref[...] = (total[...] * scale).T


def pair_blocks(left, right, w, wt, bias, cot):
    rows, cols, cz = cot.shape
    inner = HIDDEN * SEQS
    whole = lambda shape: pl.BlockSpec(shape, lambda i: (0,) * len(shape))
    flops = 2 * rows * (3 * cols * inner * cz + 2 * inner * HIDDEN * cz)
    return pl.pallas_call(
        pair_kernel,
        grid=(rows // BLOCK,),
        in_specs=[
            pl.BlockSpec((BLOCK * SEQS, HIDDEN), lambda i: (i, 0)),
            whole((cols, inner)),
            whole((HIDDEN, HIDDEN * cz)),
            whole((HIDDEN * cz, HIDDEN)),
            whole((1, cz)),
            pl.BlockSpec((BLOCK, cols, cz), lambda i: (i, 0, 0)),
        ],
        out_specs=[
            pl.BlockSpec((BLOCK, cols, cz), lambda i: (i, 0, 0)),
            pl.BlockSpec((BLOCK * SEQS, HIDDEN), lambda i: (i, 0)),
            whole((cols, inner)),
        ],
        out_shape=[
            jax.ShapeDtypeStruct((rows, cols, cz), jnp.bfloat16),
            jax.ShapeDtypeStruct((rows * SEQS, HIDDEN), jnp.float32),
            jax.ShapeDtypeStruct((cols, inner), jnp.float32),
        ],
        scratch_shapes=[
            pltpu.VMEM((inner, cols), jnp.bfloat16),
            pltpu.VMEM((inner, BLOCK * cz), jnp.bfloat16),
            pltpu.VMEM((BLOCK * SEQS, HIDDEN * cz), jnp.bfloat16),
            pltpu.VMEM((cols, BLOCK * cz), jnp.bfloat16),
            pltpu.VMEM((inner, cols), jnp.float32),
        ],
        compiler_params=pltpu.CompilerParams(
            dimension_semantics=("arbitrary",), vmem_limit_bytes=52 * 2**20),
        cost_estimate=pl.CostEstimate(
            flops=flops, bytes_accessed=4 * rows * cols * cz, transcendentals=0),
    )(left, right, w, wt, bias, cot)


def split_dot(x, weight):
    high = x.astype(jnp.bfloat16)
    low = (x - high.astype(jnp.float32)).astype(jnp.bfloat16)
    both = jnp.concatenate([high, low], axis=-1)
    return jnp.dot(both, jnp.concatenate([weight, weight], axis=0),
                   preferred_element_type=jnp.float32)


def shards(row_size, col_size, features, factor, shift, w_first, w_second,
           w_out, bias, cot):
    rows = features.shape[0]
    col = lax.axis_index("col")
    x = features.astype(jnp.float32).reshape(rows, SEQS, CHANNELS)
    center = x - jnp.mean(x, axis=-1, keepdims=True)
    inverse = lax.rsqrt(jnp.mean(center * center, axis=-1, keepdims=True) + 1e-05)
    standard = center * inverse
    normed = (standard * factor + shift).astype(jnp.bfloat16)
    right = jnp.einsum("isc,ch->ihs", normed, w_second,
                       preferred_element_type=jnp.float32).astype(jnp.bfloat16)
    right_all = lax.all_gather(right.reshape(rows, HIDDEN * SEQS), "row", axis=0, tiled=True)
    left = jnp.einsum("isc,ch->ish", normed, w_first,
                      preferred_element_type=jnp.float32).astype(jnp.bfloat16)
    cols = right_all.shape[0] // col_size
    right_use = lax.dynamic_slice_in_dim(right_all, col * cols, cols, 0)
    cz = w_out.shape[1]
    w = w_out.reshape(HIDDEN, HIDDEN * cz)
    wt = w.T
    delta, lg, rg = pair_blocks(left.reshape(rows * SEQS, HIDDEN), right_use, w, wt,
                                bias.reshape(1, cz), cot)
    half = rows // col_size
    lg = lax.psum_scatter(lg, "col", scatter_dimension=0, tiled=True)
    rg = lax.psum_scatter(rg, "row", scatter_dimension=0, tiled=True)
    moves = []
    for r in range(row_size):
        for c in range(col_size):
            chunk = c * row_size + r
            moves.append((r * col_size + c, chunk))
    rg = lax.ppermute(rg, ("row", "col"), moves)
    rg = rg.reshape(half, HIDDEN, SEQS).transpose(0, 2, 1).reshape(half * SEQS, HIDDEN)
    d = split_dot(jnp.concatenate([lg, rg], axis=-1),
                  jnp.concatenate([w_first.T, w_second.T], axis=0))
    e = d.reshape(half, SEQS, CHANNELS) * factor
    std = lax.dynamic_slice_in_dim(standard, col * half, half, 0)
    inv = lax.dynamic_slice_in_dim(inverse, col * half, half, 0)
    grad = inv * (e - jnp.mean(e, axis=-1, keepdims=True)
                  - std * jnp.mean(e * std, axis=-1, keepdims=True))
    grad = grad.astype(jnp.bfloat16).reshape(half, SEQS * CHANNELS)
    grad = lax.all_gather(grad, "col", axis=0, tiled=True)
    return delta, grad


def solution(mesh):
    in_specs = (P(("group", "row"), None), P(), P(), P(), P(), P(), P(),
                P(("group", "row"), "col", None))
    out_specs = (P(("group", "row"), "col", None), P(("group", "row"), None))
    body = functools.partial(shards, mesh.shape["row"], mesh.shape["col"])
    return jax.shard_map(body, mesh=mesh, in_specs=in_specs, out_specs=out_specs,
                         check_vma=False)
```

time: 855 us -> 209 us (0.24); the launches traced: 844 us -> 209 us
  local copies, waits for them, and re-layouts: 454 us -> 9.71 us
  matrix products: 193 us -> 2.08 us
  waiting for transfers between devices: 179 us -> 116 us
  Pallas kernels: 0 us -> 57.4 us
    reshape x20 -> x7, local copies, waits for them, and re-layouts: 325 us -> 5.14 us  [the longest x2 1.49 us: shards(): w = w_out.reshape(HIDDEN, HIDDEN * cz)]
    dot_general x44 -> x3, matrix products: 193 us -> 2.08 us  [the longest x1 0.84 us: shards(): jnp.einsum('isc,ch->ihs', normed, w_second, preferred_element_type=jnp.fl...]
    convert_element_type x10 -> x2, local copies, waits for them, and re-layouts: 118 us -> 1.59 us  [the longest x1 0.97 us: shards(): right = jnp.einsum('isc,ch->ihs', normed, w_second, preferred_element_typ...]
    psum x2 -> x0, waiting for transfers between devices: 104 us -> none  [the longest x1 84.3 us: shards(): right_block = lax.psum(right_part, 'row')]
    reduce_scatter x0 -> x2, waiting for transfers between devices: none -> 71.3 us  [the longest x1 63.1 us: shards(): rg = lax.psum_scatter(rg, 'row', scatter_dimension=0, tiled=True)]
    pallas_call x0 -> x1, Pallas kernels: none -> 57.4 us  [pair_blocks(): pl.pallas_call(pair_kernel, grid=(rows // BLOCK,), in_specs=[pl.BlockSpec...]
    all_gather x1, waiting for transfers between devices: 74.9 us -> 44 us  [shards(): lax.all_gather(right.reshape(rows, HIDDEN * SEQS), 'row', axis=0, tiled=T...]
  transfers between devices with their start and end apart: 3 -> 4, of which waited for: 3 -> 3; matrix products, arithmetic and copies ran while one was open for 0% -> 2% of each run, Pallas kernels for 0% -> 0%
where the time goes in v1:
time: 209 us
  waiting for transfers between devices  116 us (56%)
  Pallas kernels  57.4 us (27%)
  between operations  14 us (7%)
  local copies, waits for them, and re-layouts  9.71 us (5%)
  other arithmetic  6.06 us (3%)
  blocking collectives  2.09 us (1%)
    reduce_scatter x1, waiting for transfers between devices, shards(): rg = lax.psum_scatter(rg, 'row', scatter_dimension=0, tiled=True)  63.1 us
    pallas_call x1, Pallas kernels, pair_blocks(): pl.pallas_call(pair_kernel, grid=(rows // BLOCK,), in_specs=[pl.BlockSpec...  57.4 us
    all_gather x1, waiting for transfers between devices, shards(): lax.all_gather(right.reshape(rows, HIDDEN * SEQS), 'row', axis=0, tiled=T...  44 us
    reduce_scatter x1, waiting for transfers between devices, shards(): lg = lax.psum_scatter(lg, 'col', scatter_dimension=0, tiled=True)  8.25 us
  transfers between devices with their start and end apart: 4, of which 3 were waited for; matrix products, arithmetic and copies ran while one was open for 2% of the time, Pallas kernels for 0%

profile of v1, /device:TPU:0, one launch (start us, length us, event | category | flops | bytes accessed | tf_op | source)
XLA Modules:
  0.0 209.0 jit_solution(3742544086573040553)
XLA Ops:
  7.2 1.4 reshape.88
  8.7 0.5 reduce_sum.36
  9.2 0.9 multiply_reduce_fusion
  10.1 1.9 add_convert_fusion
  12.0 0.8 fusion
  12.9 1.0 copy.26
  13.8 1.5 reshape.80
  15.5 1.4 copy.27
  16.9 0.8 convolution_convert_fusion.1
  17.8 0.6 copy.24
  18.4 44.0 %all-gather.2.cloned.1.call-done = bf16[512,1536]{1,0:T(8,128)(2,1)} async-done(((bf16[64,1536]{1,0:T(8,128)(2,1)}), bf16[512,1536]{1,0:T(8,128)(2,1)}) %all-gather.2.cloned.1.call-update) | async-done | bytes 1572880 | tf_op jit(solution)/shard_map/all_gather | solution.py:128
  62.4 1.2 constant_dynamic-slice_fusion.1.right_ref
  63.6 57.4 %shard_map.95 = (bf16[64,256,128]{2,1,0:T(8,128)(2,1)}, f32[3072,32]{1,0:T(8,128)}, f32[256,1536]{1,0:T(8,128)}) custom-call(bf16[3072,32]{1,0:T(8,128)(2,1)S(1)} %bitcast.16, bf16[256,1536]{1,0:T(8,128)(2,1)S(1)} %constant_dynamic-slice_fusion.1.right_ref, bf16[32,4096]{1,0:T(8,128)(2,1)S(1)} %reshape.81.w_ref, bf16[4096,32]{1,0:T(8,128)(2,1)} %bitcast.23, ...), custom_call_target="tpu_custom_call" | custom-call | flops 20937965568 | bytes 8388608 | tf_op jit(solution)/shard_map/pallas_call | solution.py:74
  121.1 0.7 reduce-scatter.3.cloned.1.call-update
  121.8 63.1 %reduce-scatter.5.cloned.1.call-done = f32[32,1536]{1,0:T(8,128)} async-done(((f32[256,1536]{1,0:T(8,128)}), f32[32,1536]{1,0:T(8,128)}) %reduce-scatter.5.cloned.1.call-update) | async-done | bytes 196624 | tf_op jit(solution)/shard_map/reduce_scatter | solution.py:140
  184.8 1.6 collective-permute-start
  186.6 0.3 copy.28
  186.9 8.2 %reduce-scatter.3.cloned.1.call-done = f32[1536,32]{1,0:T(8,128)} async-done(((f32[3072,32]{1,0:T(8,128)}), f32[1536,32]{1,0:T(8,128)}) %reduce-scatter.3.cloned.1.call-update) | async-done | bytes 196624 | tf_op jit(solution)/shard_map/reduce_scatter | solution.py:139
  195.2 1.5 subtract_convert_fusion
  196.9 0.4 multiply_reduce_fusion.2
  197.7 0.6 copy-done.1
  198.6 0.8 multiply_convert_fusion
  199.7 2.1 all_gather.7
  201.8 0.7 copy.36
  (32 shorter events, 1.7 us)
Async XLA Ops:
  7.2 55.2 %all-gather.2.cloned.1.call-start = ((), (), s32[]{:S(2)}) async-start(), calls=%async_computation.2 | async-start | bytes 1769472 | tf_op jit(solution)/shard_map/all_gather | solution.py:128
  8.6 1.5 copy-start.6
  8.6 1.5 copy-start.7
  10.1 1.9 copy-start.5
  12.0 3.4 %copy-start.3 = (bf16[1024,128]{1,0:T(8,128)(2,1)S(1)}, bf16[1024,128]{1,0:T(8,128)(2,1)}, u32[]{:S(2)}) copy-start(bf16[1024,128]{1,0:T(8,128)(2,1)} %param.13) | copy-start | bytes 786436
  13.8 3.1 %copy-start.4 = (bf16[64,32]{0,1:T(8,128)(2,1)S(1)}, bf16[64,32]{0,1:T(8,128)(2,1)}, u32[]{:S(2)}) copy-start(bf16[64,32]{0,1:T(8,128)(2,1)} %param.11) | copy-start | bytes 12292
  15.3 169.5 %reduce-scatter.5.cloned.1.call-start = ((), (), s32[]{:S(2)}) async-start(), calls=%async_computation.4 | async-start | bytes 1769472 | tf_op jit(solution)/shard_map/reduce_scatter | solution.py:140
  17.7 45.8 %copy-start = (f32[128]{0:T(128)S(1)}, f32[128]{0:T(128)}, u32[]{:S(2)}) copy-start(f32[128]{0:T(128)} %param.14) | copy-start | bytes 1540
  121.0 74.2 %reduce-scatter.3.cloned.1.call-start = ((), (), s32[]{:S(2)}) async-start(), calls=%async_computation.3 | async-start | bytes 2359296 | tf_op jit(solution)/shard_map/reduce_scatter | solution.py:139
  184.8 1.6 collective-permute-start
  195.2 1.5 copy-start.2
  196.9 1.4 copy-start.1
Sparse Core Ops, SparseCore 0:
  15.5 46.8 all-gather.1
  121.1 63.6 reduce-scatter.4
  187.2 7.9 reduce-scatter.2

commit v2 on v1

v2 whole, which is shorter than its diff:
```python
import functools

import jax
import jax.numpy as jnp
from jax import lax
from jax.experimental import pallas as pl
from jax.experimental.pallas import tpu as pltpu
from jax.sharding import PartitionSpec as P

SEQS = 48
CHANNELS = 64
HIDDEN = 32
BLOCK = 8


def pair_kernel(row_size, col_size, left_ref, right_ref, w_ref, wt_ref, bias_ref, cot_hbm,
                out_hbm, lg_ref, rg_ref,
                right_use, right_t, z, v, cots, total, outs, rg_send, rg_recv,
                lg_send, lg_recv, cot_sem, out_sem, own_sem, gather_send, gather_recv,
                rg_send_sem, rg_recv_sem, lg_send_sem, lg_recv_sem):
    rows, cols, cz = cot_hbm.shape
    blocks = rows // BLOCK
    half_blocks = blocks // col_size
    half = rows // col_size
    owners = row_size // col_size
    scale = 1.0 / SEQS
    row = lax.axis_index("row")
    col = lax.axis_index("col")
    me = row * col_size + col
    devices = row_size * col_size
    home = row // owners
    slot = lax.rem(row, owners)

    def block_rows(index):
        return pl.ds(pl.multiple_of(index * rows, rows), rows)

    def cot_copy(i):
        at = lax.rem(i, BLOCK)
        return pltpu.make_async_copy(
            cot_hbm.at[i],
            cots.at[i // BLOCK, :, pl.ds(pl.multiple_of(at * cz, cz), cz)],
            cot_sem.at[i])

    @pl.loop(0, rows)
    def _(i):
        cot_copy(i).start()

    barrier = pltpu.get_barrier_semaphore()

    @pl.loop(1, devices)
    def _(d):
        other = lax.rem(me + d, devices)
        pl.semaphore_signal(
            barrier, inc=1,
            device_id={"row": other // col_size, "col": lax.rem(other, col_size)},
            device_id_type=pl.DeviceIdType.MESH)
    pl.semaphore_wait(barrier, devices - 1)

    def gather_copy(d):
        target = lax.rem(row + d, row_size)
        return pltpu.make_async_remote_copy(
            src_ref=right_ref, dst_ref=right_use.at[block_rows(slot)],
            send_sem=gather_send.at[d], recv_sem=gather_recv.at[slot],
            device_id={"row": target, "col": home},
            device_id_type=pl.DeviceIdType.MESH)

    def sends(d):
        return lax.rem(lax.rem(row + d, row_size), col_size) == col

    @pl.loop(1, row_size)
    def _(d):
        @pl.when(sends(d))
        def _():
            gather_copy(d).start()

    own_copy = pltpu.make_async_copy(right_ref, right_use.at[block_rows(slot)], own_sem)

    @pl.when(home == col)
    def _():
        own_copy.start()

    total[...] = jnp.zeros_like(total)
    group = 4

    @pl.loop(0, blocks)
    def _(blk):
        lefts = left_ref[pl.ds(pl.multiple_of(blk * BLOCK * SEQS, BLOCK * SEQS), BLOCK * SEQS), :]

        @pl.loop(0, HIDDEN // group)
        def _(g):
            lanes = pl.ds(pl.multiple_of(g * group * cz, group * cz), group * cz)
            part = jnp.dot(lefts, w_ref[:, lanes],
                           preferred_element_type=jnp.float32).astype(jnp.bfloat16)
            for b in range(group):
                at = pl.ds(pl.multiple_of((g * group + b) * SEQS, SEQS), SEQS)
                for i in range(BLOCK):
                    z[blk, at, i * cz:(i + 1) * cz] = part[
                        i * SEQS:(i + 1) * SEQS, b * cz:(b + 1) * cz]

        @pl.loop(0, BLOCK)
        def _(i):
            cot_copy(blk * BLOCK + i).wait()

        total[...] += lax.dot_general(z[blk], cots[blk], (((1,), (1,)), ((), ())),
                                      preferred_element_type=jnp.float32)

    rg_send[...] = (total[...] * scale).T.astype(jnp.bfloat16)

    def rg_rows(q):
        return pl.ds(pl.multiple_of(q * half, half), half)

    def rg_copy(d):
        q = lax.rem(row + d, row_size)
        target = col * row_size + q
        copy = pltpu.make_async_remote_copy(
            src_ref=rg_send.at[rg_rows(q)], dst_ref=rg_recv.at[row],
            send_sem=rg_send_sem.at[d], recv_sem=rg_recv_sem.at[row],
            device_id={"row": target // col_size, "col": lax.rem(target, col_size)},
            device_id_type=pl.DeviceIdType.MESH)
        return q, target != me, copy

    @pl.loop(0, row_size)
    def _(d):
        q, away, copy = rg_copy(d)

        @pl.when(away)
        def _():
            copy.start()

        @pl.when(jnp.logical_not(away))
        def _():
            rg_recv[row] = rg_send[rg_rows(q), :]

    @pl.when(home == col)
    def _():
        own_copy.wait()

    @pl.loop(0, owners)
    def _(k):
        @pl.when(col * owners + k != row)
        def _():
            pltpu.make_async_remote_copy(
                src_ref=right_ref, dst_ref=right_use.at[block_rows(k)],
                send_sem=gather_send.at[0], recv_sem=gather_recv.at[k],
                device_id={"row": row, "col": col},
                device_id_type=pl.DeviceIdType.MESH).wait_recv()

    right_t[...] = right_use[...].T

    def out_copy(blk, at):
        return pltpu.make_async_copy(
            outs.at[at],
            out_hbm.at[pl.ds(pl.multiple_of(blk * BLOCK, BLOCK), BLOCK)], out_sem.at[at])

    def lg_copy(t):
        return pltpu.make_async_remote_copy(
            src_ref=lg_send.at[t], dst_ref=lg_recv.at[t],
            send_sem=lg_send_sem.at[t], recv_sem=lg_recv_sem.at[t],
            device_id={"row": row, "col": 1 - col},
            device_id_type=pl.DeviceIdType.MESH)

    @pl.loop(0, blocks)
    def _(t):
        blk = lax.rem(t + (1 - col) * half_blocks, blocks)
        at = lax.rem(t, 2)

        @pl.when(t >= 2)
        def _():
            out_copy(blk, at).wait()

        @pl.loop(0, BLOCK // 2)
        def _(p):
            lanes = pl.ds(pl.multiple_of(p * 2 * cz, 2 * cz), 2 * cz)
            res = jnp.dot(right_use[...], z[blk, :, lanes],
                          preferred_element_type=jnp.float32) * scale
            for q in range(2):
                outs[at, 2 * p + q] = (res[:, q * cz:(q + 1) * cz]
                                       + bias_ref[...]).astype(jnp.bfloat16)
            u = jnp.dot(right_t[...], cots[blk, :, lanes],
                        preferred_element_type=jnp.float32).astype(jnp.bfloat16)
            for q in range(2):
                to = pl.ds(pl.multiple_of((2 * p + q) * SEQS, SEQS), SEQS)
                for b in range(HIDDEN):
                    v[to, b * cz:(b + 1) * cz] = u[
                        b * SEQS:(b + 1) * SEQS, q * cz:(q + 1) * cz]

        out_copy(blk, at).start()
        lg = jnp.dot(v[...], wt_ref[...], preferred_element_type=jnp.float32) * scale

        @pl.when(t < half_blocks)
        def _():
            lg_send[t] = lg
            lg_copy(t).start()

        @pl.when(t >= half_blocks)
        def _():
            lg_ref[t - half_blocks] = lg

    @pl.loop(0, half_blocks)
    def _(t):
        lg_copy(t).wait_recv()
        lg_ref[t] += lg_recv[t]

    for at in range(2):
        out_copy(0, at).wait()

    @pl.loop(0, row_size)
    def _(k):
        source = k * col_size + home

        @pl.when(source != me)
        def _():
            pltpu.make_async_remote_copy(
                src_ref=rg_send.at[rg_rows(0)], dst_ref=rg_recv.at[k],
                send_sem=rg_send_sem.at[0], recv_sem=rg_recv_sem.at[k],
                device_id={"row": row, "col": col},
                device_id_type=pl.DeviceIdType.MESH).wait_recv()

    summed = rg_recv[0].astype(jnp.float32)
    for k in range(1, row_size):
        summed = summed + rg_recv[k].astype(jnp.float32)
    rg_ref[...] = summed

    @pl.loop(1, row_size)
    def _(d):
        @pl.when(sends(d))
        def _():
            gather_copy(d).wait_send()

    @pl.loop(0, row_size)
    def _(d):
        q, away, copy = rg_copy(d)

        @pl.when(away)
        def _():
            copy.wait_send()

    @pl.loop(0, half_blocks)
    def _(t):
        lg_copy(t).wait_send()


def pair_blocks(row_size, col_size, left, right, w, wt, bias, cot):
    rows, cols, cz = cot.shape
    inner = HIDDEN * SEQS
    blocks = rows // BLOCK
    half_blocks = blocks // col_size
    half = rows // col_size
    flops = 2 * rows * (3 * cols * inner * cz + 2 * inner * HIDDEN * cz)
    vmem = pl.BlockSpec(memory_space=pltpu.VMEM)
    hbm = pl.BlockSpec(memory_space=pl.ANY)
    dma = pltpu.SemaphoreType.DMA
    return pl.pallas_call(
        functools.partial(pair_kernel, row_size, col_size),
        in_specs=[vmem, vmem, vmem, vmem, vmem, hbm],
        out_specs=[hbm, vmem, vmem],
        out_shape=[
            jax.ShapeDtypeStruct((rows, cols, cz), jnp.bfloat16),
            jax.ShapeDtypeStruct((half_blocks, BLOCK * SEQS, HIDDEN), jnp.float32),
            jax.ShapeDtypeStruct((half, inner), jnp.float32),
        ],
        scratch_shapes=[
            pltpu.VMEM((cols, inner), jnp.bfloat16),
            pltpu.VMEM((inner, cols), jnp.bfloat16),
            pltpu.VMEM((blocks, inner, BLOCK * cz), jnp.bfloat16),
            pltpu.VMEM((BLOCK * SEQS, HIDDEN * cz), jnp.bfloat16),
            pltpu.VMEM((blocks, cols, BLOCK * cz), jnp.bfloat16),
            pltpu.VMEM((inner, cols), jnp.float32),
            pltpu.VMEM((2, BLOCK, cols, cz), jnp.bfloat16),
            pltpu.VMEM((cols, inner), jnp.bfloat16),
            pltpu.VMEM((row_size, half, inner), jnp.bfloat16),
            pltpu.VMEM((half_blocks, BLOCK * SEQS, HIDDEN), jnp.float32),
            pltpu.VMEM((half_blocks, BLOCK * SEQS, HIDDEN), jnp.float32),
            dma((rows,)), dma((2,)), dma,
            dma((row_size,)), dma((row_size // col_size,)),
            dma((row_size,)), dma((row_size,)),
            dma((half_blocks,)), dma((half_blocks,)),
        ],
        compiler_params=pltpu.CompilerParams(
            collective_id=0, has_side_effects=True, vmem_limit_bytes=62 * 2**20),
        cost_estimate=pl.CostEstimate(
            flops=flops, bytes_accessed=4 * rows * cols * cz, transcendentals=0),
    )(left, right, w, wt, bias, cot)


def split_dot(x, weight):
    high = x.astype(jnp.bfloat16)
    low = (x - high.astype(jnp.float32)).astype(jnp.bfloat16)
    both = jnp.concatenate([high, low], axis=-1)
    return jnp.dot(both, jnp.concatenate([weight, weight], axis=0),
                   preferred_element_type=jnp.float32)


def shards(row_size, col_size, features, factor, shift, w_first, w_second,
           w_out, bias, cot):
    rows = features.shape[0]
    col = lax.axis_index("col")
    x = features.astype(jnp.float32).reshape(rows, SEQS, CHANNELS)
    center = x - jnp.mean(x, axis=-1, keepdims=True)
    inverse = lax.rsqrt(jnp.mean(center * center, axis=-1, keepdims=True) + 1e-05)
    standard = center * inverse
    normed = (standard * factor + shift).astype(jnp.bfloat16)
    right = jnp.einsum("isc,ch->ihs", normed, w_second,
                       preferred_element_type=jnp.float32).astype(jnp.bfloat16)
    left = jnp.einsum("isc,ch->ish", normed, w_first,
                      preferred_element_type=jnp.float32).astype(jnp.bfloat16)
    cz = w_out.shape[1]
    w = w_out.reshape(HIDDEN, HIDDEN * cz)
    wt = w.T
    delta, lg, rg = pair_blocks(
        row_size, col_size, left.reshape(rows * SEQS, HIDDEN),
        right.reshape(rows, HIDDEN * SEQS), w, wt, bias.reshape(1, cz), cot)
    half = rows // col_size
    lg = lg.reshape(half * SEQS, HIDDEN)
    rg = rg.reshape(half, HIDDEN, SEQS).transpose(0, 2, 1).reshape(half * SEQS, HIDDEN)
    d = split_dot(jnp.concatenate([lg, rg], axis=-1),
                  jnp.concatenate([w_first.T, w_second.T], axis=0))
    e = d.reshape(half, SEQS, CHANNELS) * factor
    std = lax.dynamic_slice_in_dim(standard, col * half, half, 0)
    inv = lax.dynamic_slice_in_dim(inverse, col * half, half, 0)
    grad = inv * (e - jnp.mean(e, axis=-1, keepdims=True)
                  - std * jnp.mean(e * std, axis=-1, keepdims=True))
    grad = grad.astype(jnp.bfloat16).reshape(half, SEQS * CHANNELS)
    grad = lax.all_gather(grad, "col", axis=0, tiled=True)
    return delta, grad


def solution(mesh):
    in_specs = (P(("group", "row"), None), P(), P(), P(), P(), P(), P(),
                P(("group", "row"), "col", None))
    out_specs = (P(("group", "row"), "col", None), P(("group", "row"), None))
    body = functools.partial(shards, mesh.shape["row"], mesh.shape["col"])
    return jax.shard_map(body, mesh=mesh, in_specs=in_specs, out_specs=out_specs,
                         check_vma=False)
```

time: 209 us -> 91.5 us (0.44)
  waiting for transfers between devices: 116 us -> 0 us
  between operations: 14 us -> 0.83 us
  Pallas kernels: 57.4 us -> 66.3 us
  local copies, waits for them, and re-layouts: 9.71 us -> 15.7 us
    reduce_scatter x2 -> x0, waiting for transfers between devices: 71.3 us -> none  [the longest x1 63.1 us: shards(): rg = lax.psum_scatter(rg, 'row', scatter_dimension=0, tiled=True)]
    all_gather x1 -> x0, waiting for transfers between devices: 44 us -> none  [shards(): lax.all_gather(right.reshape(rows, HIDDEN * SEQS), 'row', axis=0, tiled=T...]
    pallas_call x1, Pallas kernels: 57.4 us -> 66.3 us  [pair_blocks(): pl.pallas_call(functools.partial(pair_kernel, row_size, col_size), in_spe...]
    unnamed x17 -> x18, local copies, waits for them, and re-layouts: 1.43 us -> 6.29 us
  transfers between devices with their start and end apart: 4 -> 0, of which waited for: 3 -> 0; matrix products, arithmetic and copies ran while one was open for 2% -> 0% of each run, Pallas kernels for 0% -> 0%
where the time goes in v2:
time: 91.5 us; the launch traced here: 91.2 us
  Pallas kernels  66.3 us (72%)
  local copies, waits for them, and re-layouts  15.7 us (17%)
  other arithmetic  4.38 us (5%)
  blocking collectives  2.09 us (2%)
  matrix products  1.93 us (2%)
    pallas_call x1, Pallas kernels, pair_blocks(): pl.pallas_call(functools.partial(pair_kernel, row_size, col_size), in_spe...  66.3 us
    unnamed x18, local copies, waits for them, and re-layouts  6.29 us
    all_gather x1, blocking collectives, shards(): grad = lax.all_gather(grad, 'col', axis=0, tiled=True)  2.09 us
    convert_element_type x1, other arithmetic, shards(): normed = (standard * factor + shift).astype(jnp.bfloat16)  1.86 us

profile of v2, /device:TPU:0, one launch (start us, length us, event | category | flops | bytes accessed | tf_op | source)
XLA Modules:
  0.0 91.2 jit_solution(8353662973753613650)
XLA Ops:
  0.6 1.4 %reshape.92 = f32[64,48,64]{2,1,0:T(8,128)S(1)} reshape(bf16[64,3072]{1,0:T(8,128)(2,1)} %param.8) | data formatting | bytes 1179648 | tf_op jit(solution)/shard_map/reshape | solution.py:298
  2.1 0.5 reduce_sum.36
  2.6 0.9 multiply_reduce_fusion
  3.5 1.9 %add_convert_fusion = (bf16[64,48,64]{2,1,0:T(8,128)(2,1)S(1)}, f32[64,48,64]{2,1,0:T(8,128)}) fusion(f32[64]{0:T(128)S(1)} %copy-done.7, f32[64]{0:T(128)S(1)} %copy-done.6, f32[64,48]{1,0:T(8,128)S(1)} %add_rsqrt_fusion, f32[64,48,64]{2,1,0:T(8,128)S(1)} %reshape.92, f32[64,48]{1,0:T(8,128)S(1)} %broadcast_multiply_fusion), kind=kLoop, calls=%fused_computation | loop fusion | flops 983040 | bytes 1991168 | tf_op jit(solution)/shard_map/convert_element_type | solution.py:302
  5.4 0.8 convolution_convert_fusion.1
  6.2 1.5 %copy.24 = bf16[64,48,32]{2,1,0:T(8,128)(2,1)} copy(bf16[64,48,32]{0,2,1:T(8,128)(2,1)S(1)} %convolution_convert_fusion.1) | data formatting | bytes 393216 | tf_op jit(solution)/shard_map/convert_element_type | solution.py:306
  7.7 0.8 fusion
  8.6 1.0 %copy.26 = bf16[64,32,48]{2,1,0:T(8,128)(2,1)S(1)} copy(bf16[64,32,48]{0,1,2:T(8,128)(2,1)S(1)} %fusion) | data formatting | bytes 393216 | tf_op jit(solution)/shard_map/convert_element_type | solution.py:304
  9.6 1.5 %reshape.83.right_ref = bf16[64,1536]{1,0:T(8,128)(2,1)} reshape(bf16[64,32,48]{2,1,0:T(8,128)(2,1)S(1)} %copy.26) | data formatting | bytes 393216 | tf_op jit(solution)/shard_map/reshape | solution.py:312
  11.2 1.3 %copy.27 = bf16[32,4096]{0,1:T(8,128)(2,1)} copy(bf16[32,4096]{1,0:T(8,128)(2,1)S(1)} %reshape.84.w_ref) | data formatting | bytes 524288 | tf_op jit(solution)/shard_map/reshape | solution.py:308
  12.5 66.3 %shard_map.95 = (bf16[64,256,128]{2,1,0:T(8,128)(2,1)}, f32[4,384,32]{2,1,0:T(8,128)}, f32[32,1536]{1,0:T(8,128)}) custom-call(bf16[3072,32]{1,0:T(8,128)(2,1)} %bitcast.24, bf16[64,1536]{1,0:T(8,128)(2,1)} %reshape.83.right_ref, bf16[32,4096]{1,0:T(8,128)(2,1)} %copy-done.1, bf16[4096,32]{1,0:T(8,128)(2,1)} %bitcast.23, f32[1,128]{1,0:T(1,128)} %bitcast.28, ...), custom_call_target="tpu_custom_call" | custom-call | flops 20937965568 | bytes 8388608 | tf_op jit(solution)/shard_map/pallas_call | solution.py:253
  78.8 1.2 %reshape.87 = f32[32,32,48]{2,1,0:T(8,128)S(1)} reshape(f32[32,1536]{1,0:T(8,128)} %get-tuple-element.7) | data formatting | bytes 393216 | tf_op jit(solution)/shard_map/reshape | solution.py:315
  80.0 0.3 copy.37
  80.3 0.3 reshape.88
  80.6 0.2 copy.29
  80.9 0.3 multiply_reduce_fusion.2
  81.2 0.3 copy.31
  81.5 0.8 copy-done
  82.3 0.3 multiply_reduce_fusion.1
  82.7 0.8 multiply_convert_fusion
  83.4 0.3 reshape.90
  83.7 2.1 %all_gather.3 = bf16[64,3072]{1,0:T(8,128)(2,1)S(1)} all-gather(bf16[32,3072]{1,0:T(8,128)(2,1)S(1)} %reshape.90), channel_id=1, replica_groups=mesh['group'=2,'row'=8,'col'=2] {'col'}, dimensions={0}, use_global_device_ids=true | all-gather | bytes 589824 | tf_op jit(solution)/shard_map/all_gather | solution.py:324
  85.8 4.7 %copy.40 = bf16[64,256,128]{2,1,0:T(8,128)(2,1)} copy(bf16[64,256,128]{2,1,0:T(8,128)(2,1)} %get-tuple-element.16) | data formatting | bytes 8388608
  90.5 0.7 copy.41
  (23 shorter events, 0.3 us)
Async XLA Ops:
  2.1 1.5 %copy-start.6 = (f32[64]{0:T(128)S(1)}, f32[64]{0:T(128)}, u32[]{:S(2)}) copy-start(f32[64]{0:T(128)} %param.9) | copy-start | bytes 772
  2.1 1.5 %copy-start.7 = (f32[64]{0:T(128)S(1)}, f32[64]{0:T(128)}, u32[]{:S(2)}) copy-start(f32[64]{0:T(128)} %param.10) | copy-start | bytes 772
  3.5 1.9 %copy-start.4 = (bf16[64,32]{0,1:T(8,128)(2,1)S(1)}, bf16[64,32]{0,1:T(8,128)(2,1)}, u32[]{:S(2)}) copy-start(bf16[64,32]{0,1:T(8,128)(2,1)} %param.11) | copy-start | bytes 12292
  5.4 2.3 %copy-start.5 = (bf16[64,32]{0,1:T(8,128)(2,1)S(1)}, bf16[64,32]{0,1:T(8,128)(2,1)}, u32[]{:S(2)}) copy-start(bf16[64,32]{0,1:T(8,128)(2,1)} %param.12) | copy-start | bytes 12292
  7.7 3.3 %copy-start.3 = (bf16[1024,128]{1,0:T(8,128)(2,1)S(1)}, bf16[1024,128]{1,0:T(8,128)(2,1)}, u32[]{:S(2)}) copy-start(bf16[1024,128]{1,0:T(8,128)(2,1)} %param.13) | copy-start | bytes 786436
  11.1 1.3 %copy-start.1 = (bf16[32,4096]{1,0:T(8,128)(2,1)}, bf16[32,4096]{1,0:T(8,128)(2,1)S(1)}, u32[]{:S(2)}) copy-start(bf16[32,4096]{1,0:T(8,128)(2,1)S(1)} %reshape.84.w_ref) | copy-start | bytes 786436
  78.8 1.8 %copy-start.2 = (f32[4,384,32]{2,1,0:T(8,128)S(1)}, f32[4,384,32]{2,1,0:T(8,128)}, u32[]{:S(2)}) copy-start(f32[4,384,32]{2,1,0:T(8,128)} %get-tuple-element.6) | copy-start | bytes 589828
  80.8 1.4 %copy-start = (f32[64,48,64]{2,1,0:T(8,128)S(1)}, f32[64,48,64]{2,1,0:T(8,128)}, u32[]{:S(2)}) copy-start(f32[64,48,64]{2,1,0:T(8,128)} %get-tuple-element.9) | copy-start | bytes 2359300

commit v3 on v2

--- a/solution.py
+++ b/solution.py
@@ -11,11 +11,13 @@
 CHANNELS = 64
 HIDDEN = 32
 BLOCK = 8
-
-
-def pair_kernel(row_size, col_size, left_ref, right_ref, w_ref, wt_ref, bias_ref, cot_hbm,
+Z_GROUP = 8
+U_GROUP = 4
+
+
+def pair_kernel(row_size, col_size, left_ref, right_ref, w_ref, bias_ref, cot_hbm,
                 out_hbm, lg_ref, rg_ref,
-                right_use, right_t, z, v, cots, total, outs, rg_send, rg_recv,
+                right_use, right_t, z, cots, total, outs, rg_send, rg_recv,
                 lg_send, lg_recv, cot_sem, out_sem, own_sem, gather_send, gather_recv,
                 rg_send_sem, rg_recv_sem, lg_send_sem, lg_recv_sem):
     rows, cols, cz = cot_hbm.shape
@@ -80,21 +82,18 @@
         own_copy.start()
 
     total[...] = jnp.zeros_like(total)
-    group = 4
 
     @pl.loop(0, blocks)
     def _(blk):
         lefts = left_ref[pl.ds(pl.multiple_of(blk * BLOCK * SEQS, BLOCK * SEQS), BLOCK * SEQS), :]
 
-        @pl.loop(0, HIDDEN // group)
-        def _(g):
-            lanes = pl.ds(pl.multiple_of(g * group * cz, group * cz), group * cz)
-            part = jnp.dot(lefts, w_ref[:, lanes],
+        for g in range(0, HIDDEN, Z_GROUP):
+            part = jnp.dot(lefts, w_ref[:, g * cz:(g + Z_GROUP) * cz],
                            preferred_element_type=jnp.float32).astype(jnp.bfloat16)
-            for b in range(group):
-                at = pl.ds(pl.multiple_of((g * group + b) * SEQS, SEQS), SEQS)
+            for b in range(Z_GROUP):
+                at = (g + b) * SEQS
                 for i in range(BLOCK):
-                    z[blk, at, i * cz:(i + 1) * cz] = part[
+                    z[blk, at:at + SEQS, i * cz:(i + 1) * cz] = part[
                         i * SEQS:(i + 1) * SEQS, b * cz:(b + 1) * cz]
 
         @pl.loop(0, BLOCK)
@@ -168,24 +167,24 @@
         def _():
             out_copy(blk, at).wait()
 
-        @pl.loop(0, BLOCK // 2)
-        def _(p):
-            lanes = pl.ds(pl.multiple_of(p * 2 * cz, 2 * cz), 2 * cz)
-            res = jnp.dot(right_use[...], z[blk, :, lanes],
-                          preferred_element_type=jnp.float32) * scale
-            for q in range(2):
-                outs[at, 2 * p + q] = (res[:, q * cz:(q + 1) * cz]
-                                       + bias_ref[...]).astype(jnp.bfloat16)
-            u = jnp.dot(right_t[...], cots[blk, :, lanes],
+        res = jnp.dot(right_use[...], z[blk], preferred_element_type=jnp.float32) * scale
+        for i in range(BLOCK):
+            outs[at, i] = (res[:, i * cz:(i + 1) * cz] + bias_ref[...]).astype(jnp.bfloat16)
+        out_copy(blk, at).start()
+
+        lg = jnp.zeros((BLOCK * SEQS, HIDDEN), jnp.float32)
+        for g in range(0, HIDDEN, U_GROUP):
+            u = jnp.dot(right_t[g * SEQS:(g + U_GROUP) * SEQS], cots[blk],
                         preferred_element_type=jnp.float32).astype(jnp.bfloat16)
-            for q in range(2):
-                to = pl.ds(pl.multiple_of((2 * p + q) * SEQS, SEQS), SEQS)
-                for b in range(HIDDEN):
-                    v[to, b * cz:(b + 1) * cz] = u[
-                        b * SEQS:(b + 1) * SEQS, q * cz:(q + 1) * cz]
-
-        out_copy(blk, at).start()
-        lg = jnp.dot(v[...], wt_ref[...], preferred_element_type=jnp.float32) * scale
+            u = jnp.concatenate([
+                jnp.concatenate([
+                    u[b * SEQS:(b + 1) * SEQS, i * cz:(i + 1) * cz]
+                    for b in range(U_GROUP)], axis=1)
+                for i in range(BLOCK)], axis=0)
+            lg = lg + lax.dot_general(
+                u, w_ref[:, g * cz:(g + U_GROUP) * cz], (((1,), (1,)), ((), ())),
+                preferred_element_type=jnp.float32)
+        lg = lg * scale
 
         @pl.when(t < half_blocks)
         def _():
@@ -240,7 +239,7 @@
         lg_copy(t).wait_send()
 
 
-def pair_blocks(row_size, col_size, left, right, w, wt, bias, cot):
+def pair_blocks(row_size, col_size, left, right, w, bias, cot):
     rows, cols, cz = cot.shape
     inner = HIDDEN * SEQS
     blocks = rows // BLOCK
@@ -252,7 +251,7 @@
     dma = pltpu.SemaphoreType.DMA
     return pl.pallas_call(
         functools.partial(pair_kernel, row_size, col_size),
-        in_specs=[vmem, vmem, vmem, vmem, vmem, hbm],
+        in_specs=[vmem, vmem, vmem, vmem, hbm],
         out_specs=[hbm, vmem, vmem],
         out_shape=[
             jax.ShapeDtypeStruct((rows, cols, cz), jnp.bfloat16),
@@ -263,7 +262,6 @@
             pltpu.VMEM((cols, inner), jnp.bfloat16),
             pltpu.VMEM((inner, cols), jnp.bfloat16),
             pltpu.VMEM((blocks, inner, BLOCK * cz), jnp.bfloat16),
-            pltpu.VMEM((BLOCK * SEQS, HIDDEN * cz), jnp.bfloat16),
             pltpu.VMEM((blocks, cols, BLOCK * cz), jnp.bfloat16),
             pltpu.VMEM((inner, cols), jnp.float32),
             pltpu.VMEM((2, BLOCK, cols, cz), jnp.bfloat16),
@@ -280,7 +278,7 @@
             collective_id=0, has_side_effects=True, vmem_limit_bytes=62 * 2**20),
         cost_estimate=pl.CostEstimate(
             flops=flops, bytes_accessed=4 * rows * cols * cz, transcendentals=0),
-    )(left, right, w, wt, bias, cot)
+    )(left, right, w, bias, cot)
 
 
 def split_dot(x, weight):
@@ -302,14 +300,13 @@
     normed = (standard * factor + shift).astype(jnp.bfloat16)
     right = jnp.einsum("isc,ch->ihs", normed, w_second,
                        preferred_element_type=jnp.float32).astype(jnp.bfloat16)
-    left = jnp.einsum("isc,ch->ish", normed, w_first,
-                      preferred_element_type=jnp.float32).astype(jnp.bfloat16)
+    left = jnp.dot(normed.reshape(rows * SEQS, CHANNELS), w_first,
+                   preferred_element_type=jnp.float32).astype(jnp.bfloat16)
     cz = w_out.shape[1]
     w = w_out.reshape(HIDDEN, HIDDEN * cz)
-    wt = w.T
     delta, lg, rg = pair_blocks(
-        row_size, col_size, left.reshape(rows * SEQS, HIDDEN),
-        right.reshape(rows, HIDDEN * SEQS), w, wt, bias.reshape(1, cz), cot)
+        row_size, col_size, left,
+        right.reshape(rows, HIDDEN * SEQS), w, bias.reshape(1, cz), cot)
     half = rows // col_size
     lg = lg.reshape(half * SEQS, HIDDEN)
     rg = rg.reshape(half, HIDDEN, SEQS).transpose(0, 2, 1).reshape(half * SEQS, HIDDEN)

time: 91.5 us -> 81 us (0.89)
  Pallas kernels: 66.3 us -> 51.6 us
  matrix products: 1.93 us -> 5.17 us
  local copies, waits for them, and re-layouts: 15.7 us -> 17.3 us
    pallas_call x1, Pallas kernels: 66.3 us -> 51.6 us  [pair_blocks(): pl.pallas_call(functools.partial(pair_kernel, row_size, col_size), in_spe...]
    dot_general x1, matrix products: 0.84 us -> 4.08 us  [shards(): jnp.dot(normed.reshape(rows * SEQS, CHANNELS), w_first, preferred_element...]
    reshape x1, local copies, waits for them, and re-layouts: 0.24 us -> 1.37 us  [shards(): lg = lg.reshape(half * SEQS, HIDDEN)]
    unnamed x18 -> x26, local copies, waits for them, and re-layouts: 6.29 us -> 5.7 us
    reshape x1 -> x2, local copies, waits for them, and re-layouts: 1.42 us -> 1.84 us  [shards(): x = features.astype(jnp.float32).reshape(rows, SEQS, CHANNELS)]
where the time goes in v3:
time: 81 us; the launch traced here: 80.6 us
  Pallas kernels  51.6 us (64%)
  local copies, waits for them, and re-layouts  17.3 us (21%)
  matrix products  5.17 us (6%)
  other arithmetic  3.51 us (4%)
  blocking collectives  2.09 us (3%)
  between operations  0.92 us (1%)
    pallas_call x1, Pallas kernels, pair_blocks(): pl.pallas_call(functools.partial(pair_kernel, row_size, col_size), in_spe...  51.6 us
    unnamed x26, local copies, waits for them, and re-layouts  5.7 us
    dot_general x1, matrix products, shards(): jnp.dot(normed.reshape(rows * SEQS, CHANNELS), w_first, preferred_element...  4.08 us
    all_gather x1, blocking collectives, shards(): grad = lax.all_gather(grad, 'col', axis=0, tiled=True)  2.09 us
    convert_element_type x1, local copies, waits for them, and re-layouts, shards(): left = jnp.dot(normed.reshape(rows * SEQS, CHANNELS), w_first, preferred_...  2.08 us
    reshape x2, local copies, waits for them, and re-layouts, shards(): x = features.astype(jnp.float32).reshape(rows, SEQS, CHANNELS)  1.84 us
    reshape x3, local copies, waits for them, and re-layouts, shards(): rg.reshape(half, HIDDEN, SEQS).transpose(0, 2, 1)  1.73 us

profile of v3, /device:TPU:0, one launch (start us, length us, event | category | flops | bytes accessed | tf_op | source)
XLA Modules:
  0.0 80.6 jit_solution(5047773924284828653)
XLA Ops:
  0.6 1.4 %reshape.92 = f32[64,48,64]{2,1,0:T(8,128)S(1)} reshape(bf16[64,3072]{1,0:T(8,128)(2,1)} %param.8) | data formatting | bytes 1179648 | tf_op jit(solution)/shard_map/reshape | solution.py:296
  2.1 0.5 reduce_sum.36
  2.6 0.9 %multiply_reduce_fusion = f32[64,48]{1,0:T(8,128)S(1)} fusion(f32[64,48,64]{2,1,0:T(8,128)S(1)} %reshape.92, f32[64,48]{1,0:T(8,128)S(1)} %broadcast_multiply_fusion), kind=kLoop, calls=%fused_computation.3 | loop fusion | flops 586752 | bytes 811008 | tf_op jit(solution)/shard_map/reduce_sum | solution.py:298
  3.6 1.0 %add_convert_fusion = (bf16[64,48,64]{2,1,0:T(8,128)(2,1)S(1)}, f32[64,48,64]{2,1,0:T(8,128)S(1)}) fusion(f32[64]{0:T(128)S(1)} %copy-done.10, f32[64]{0:T(128)S(1)} %copy-done.9, f32[64,48]{1,0:T(8,128)S(1)} %add_rsqrt_fusion, f32[64,48,64]{2,1,0:T(8,128)S(1)} %reshape.92, f32[64,48]{1,0:T(8,128)S(1)} %broadcast_multiply_fusion), kind=kLoop, calls=%fused_computation.1 | loop fusion | flops 983040 | bytes 1991168 | tf_op jit(solution)/shard_map/convert_element_type | solution.py:300
  4.6 0.8 %fusion = bf16[64,32,48]{0,1,2:T(8,128)(2,1)S(1)} fusion(bf16[64,48,64]{2,1,0:T(8,128)(2,1)S(1)} %get-tuple-element.8, bf16[64,32]{0,1:T(8,128)(2,1)S(1)} %copy-done.7), kind=kOutput, calls=%fused_computation.6 | convolution fusion | flops 12681216 | bytes 593920 | tf_op jit(solution)/shard_map/isc,ch->ihs/dot_general | solution.py:301
  5.5 1.0 %copy.27 = bf16[64,32,48]{2,1,0:T(8,128)(2,1)S(1)} copy(bf16[64,32,48]{0,1,2:T(8,128)(2,1)S(1)} %fusion) | data formatting | bytes 393216 | tf_op jit(solution)/shard_map/convert_element_type | solution.py:302
  6.4 1.5 %reshape.93.right_ref = bf16[64,1536]{1,0:T(8,128)(2,1)} reshape(bf16[64,32,48]{2,1,0:T(8,128)(2,1)S(1)} %copy.27) | data formatting | bytes 393216 | tf_op jit(solution)/shard_map/reshape | solution.py:309
  8.0 0.7 div.17
  8.7 0.4 reshape.91
  9.1 4.1 %convolution_convert_fusion = bf16[3072,32]{0,1:T(8,128)(2,1)} fusion(bf16[64,32]{0,1:T(8,128)(2,1)} %param.11, f32[3072,64]{1,0:T(8,128)S(1)} %reshape.91, f32[64]{0:T(128)} %param.10, f32[64]{0:T(128)S(1)} %copy-done.9, f32[3072]{0:T(1024)S(1)} %rsqrt.18, f32[3072]{0:T(1024)} %div.17), kind=kOutput, calls=%fused_computation | convolution fusion | flops 13664256 | bytes 1012224 | tf_op jit(solution)/shard_map/dot_general | solution.py:303
  13.2 2.1 %copy.28.left_ref = bf16[3072,32]{1,0:T(8,128)(2,1)} copy(bf16[3072,32]{0,1:T(8,128)(2,1)} %convolution_convert_fusion) | data formatting | bytes 393216 | tf_op jit(solution)/shard_map/convert_element_type | solution.py:304
  15.3 0.8 %reshape.94.w_ref = bf16[32,4096]{1,0:T(8,128)(2,1)} reshape(bf16[1024,128]{1,0:T(8,128)(2,1)S(1)} %copy-done.6) | data formatting | bytes 524288 | tf_op jit(solution)/shard_map/reshape | solution.py:306
  16.1 51.6 %shard_map.95 = (bf16[64,256,128]{2,1,0:T(8,128)(2,1)}, f32[4,384,32]{2,1,0:T(8,128)}, f32[32,1536]{1,0:T(8,128)}) custom-call(bf16[3072,32]{1,0:T(8,128)(2,1)} %copy.28.left_ref, bf16[64,1536]{1,0:T(8,128)(2,1)} %reshape.93.right_ref, bf16[32,4096]{1,0:T(8,128)(2,1)} %reshape.94.w_ref, f32[1,128]{1,0:T(1,128)} %bitcast.22, bf16[64,256,128]{2,1,0:T(8,128)(2,1)} %cot_hbm.1), custom_call_target="tpu_custom_call" | custom-call | flops 20937965568 | bytes 8388608 | tf_op jit(solution)/shard_map/pallas_call | solution.py:252
  67.7 1.2 %reshape.97 = f32[32,32,48]{2,1,0:T(8,128)S(1)} reshape(f32[32,1536]{1,0:T(8,128)} %get-tuple-element.7) | data formatting | bytes 393216 | tf_op jit(solution)/shard_map/reshape | solution.py:312
  68.8 0.3 copy.36
  69.2 0.3 reshape.98
  69.4 1.4 %copy.30 = f32[1536,32]{0,1:T(8,128)S(1)} copy(f32[1536,32]{1,0:T(8,128)} %bitcast.19) | data formatting | bytes 393216 | tf_op jit(solution)/shard_map/reshape | solution.py:311
  71.2 0.3 copy.32
  71.5 0.3 multiply_reduce_fusion.1
  72.0 0.8 multiply_convert_fusion
  72.8 0.3 reshape.100
  73.1 2.1 %all_gather.3 = bf16[64,3072]{1,0:T(8,128)(2,1)S(1)} all-gather(bf16[32,3072]{1,0:T(8,128)(2,1)S(1)} %reshape.100), channel_id=1, replica_groups=mesh['group'=2,'row'=8,'col'=2] {'col'}, dimensions={0}, use_global_device_ids=true | all-gather | bytes 589824 | tf_op jit(solution)/shard_map/all_gather | solution.py:321
  75.1 4.7 %copy.39 = bf16[64,256,128]{2,1,0:T(8,128)(2,1)} copy(bf16[64,256,128]{2,1,0:T(8,128)(2,1)} %get-tuple-element.16) | data formatting | bytes 8388608
  79.8 0.7 copy.40
  (33 shorter events, 0.7 us)
Async XLA Ops:
  2.1 1.5 %copy-start.9 = (f32[64]{0:T(128)S(1)}, f32[64]{0:T(128)}, u32[]{:S(2)}) copy-start(f32[64]{0:T(128)} %param.9) | copy-start | bytes 772
  2.1 1.5 %copy-start.10 = (f32[64]{0:T(128)S(1)}, f32[64]{0:T(128)}, u32[]{:S(2)}) copy-start(f32[64]{0:T(128)} %param.10) | copy-start | bytes 772
  2.6 2.0 %copy-start.1 = (f32[64,48]{1,0:T(8,128)}, f32[64,48]{1,0:T(8,128)S(1)}, u32[]{:S(2)}) copy-start(f32[64,48]{1,0:T(8,128)S(1)} %broadcast_multiply_fusion) | copy-start | bytes 36868
  3.5 1.0 %copy-start.3 = (f32[64,48]{1,0:T(8,128)}, f32[64,48]{1,0:T(8,128)S(1)}, u32[]{:S(2)}) copy-start(f32[64,48]{1,0:T(8,128)S(1)} %add_rsqrt_fusion) | copy-start | bytes 36868
  3.6 1.0 %copy-start.7 = (bf16[64,32]{0,1:T(8,128)(2,1)S(1)}, bf16[64,32]{0,1:T(8,128)(2,1)}, u32[]{:S(2)}) copy-start(bf16[64,32]{0,1:T(8,128)(2,1)} %param.12) | copy-start | bytes 12292
  4.6 4.1 %copy-start = (bf16[64,3072]{1,0:T(8,128)(2,1)S(1)}, bf16[64,3072]{1,0:T(8,128)(2,1)}, u32[]{:S(2)}) copy-start(bf16[64,3072]{1,0:T(8,128)(2,1)} %param.8) | copy-start | bytes 1179652
  4.6 3.3 %copy-start.4 = (f32[64,48]{1,0:T(8,128)S(1)}, f32[64,48]{1,0:T(8,128)}, u32[]{:S(2)}) copy-start(f32[64,48]{1,0:T(8,128)} %copy-done.3) | copy-start | bytes 36868
  4.6 3.4 %copy-start.2 = (f32[64,48]{1,0:T(8,128)S(1)}, f32[64,48]{1,0:T(8,128)}, u32[]{:S(2)}) copy-start(f32[64,48]{1,0:T(8,128)} %copy-done.1) | copy-start | bytes 36868
  9.1 6.2 %copy-start.6 = (bf16[1024,128]{1,0:T(8,128)(2,1)S(1)}, bf16[1024,128]{1,0:T(8,128)(2,1)}, u32[]{:S(2)}) copy-start(bf16[1024,128]{1,0:T(8,128)(2,1)} %param.13) | copy-start | bytes 786436
  69.2 1.7 %copy-start.8 = (bf16[64,32]{0,1:T(8,128)(2,1)S(1)}, bf16[64,32]{0,1:T(8,128)(2,1)}, u32[]{:S(2)}) copy-start(bf16[64,32]{0,1:T(8,128)(2,1)} %param.12) | copy-start | bytes 12292
  69.2 1.7 %copy-start.11 = (bf16[64,32]{0,1:T(8,128)(2,1)S(1)}, bf16[64,32]{0,1:T(8,128)(2,1)}, u32[]{:S(2)}) copy-start(bf16[64,32]{0,1:T(8,128)(2,1)} %param.11) | copy-start | bytes 12292
  71.2 0.8 copy-start.5

commit v4 on v3

--- a/solution.py
+++ b/solution.py
@@ -15,7 +15,7 @@
 U_GROUP = 4
 
 
-def pair_kernel(row_size, col_size, left_ref, right_ref, w_ref, bias_ref, cot_hbm,
+def pair_kernel(row_size, col_size, normed_ref, first_ref, right_ref, w_ref, bias_ref, cot_hbm,
                 out_hbm, lg_ref, rg_ref,
                 right_use, right_t, z, cots, total, outs, rg_send, rg_recv,
                 lg_send, lg_recv, cot_sem, out_sem, own_sem, gather_send, gather_recv,
@@ -85,7 +85,9 @@
 
     @pl.loop(0, blocks)
     def _(blk):
-        lefts = left_ref[pl.ds(pl.multiple_of(blk * BLOCK * SEQS, BLOCK * SEQS), BLOCK * SEQS), :]
+        at = pl.ds(pl.multiple_of(blk * BLOCK * SEQS, BLOCK * SEQS), BLOCK * SEQS)
+        lefts = jnp.dot(normed_ref[at, :], first_ref[...],
+                        preferred_element_type=jnp.float32).astype(jnp.bfloat16)
 
         for g in range(0, HIDDEN, Z_GROUP):
             part = jnp.dot(lefts, w_ref[:, g * cz:(g + Z_GROUP) * cz],
@@ -239,7 +241,7 @@
         lg_copy(t).wait_send()
 
 
-def pair_blocks(row_size, col_size, left, right, w, bias, cot):
+def pair_blocks(row_size, col_size, normed, first, right, w, bias, cot):
     rows, cols, cz = cot.shape
     inner = HIDDEN * SEQS
     blocks = rows // BLOCK
@@ -251,7 +253,7 @@
     dma = pltpu.SemaphoreType.DMA
     return pl.pallas_call(
         functools.partial(pair_kernel, row_size, col_size),
-        in_specs=[vmem, vmem, vmem, vmem, hbm],
+        in_specs=[vmem, vmem, vmem, vmem, vmem, hbm],
         out_specs=[hbm, vmem, vmem],
         out_shape=[
             jax.ShapeDtypeStruct((rows, cols, cz), jnp.bfloat16),
@@ -278,7 +280,7 @@
             collective_id=0, has_side_effects=True, vmem_limit_bytes=62 * 2**20),
         cost_estimate=pl.CostEstimate(
             flops=flops, bytes_accessed=4 * rows * cols * cz, transcendentals=0),
-    )(left, right, w, bias, cot)
+    )(normed, first, right, w, bias, cot)
 
 
 def split_dot(x, weight):
@@ -300,12 +302,10 @@
     normed = (standard * factor + shift).astype(jnp.bfloat16)
     right = jnp.einsum("isc,ch->ihs", normed, w_second,
                        preferred_element_type=jnp.float32).astype(jnp.bfloat16)
-    left = jnp.dot(normed.reshape(rows * SEQS, CHANNELS), w_first,
-                   preferred_element_type=jnp.float32).astype(jnp.bfloat16)
     cz = w_out.shape[1]
     w = w_out.reshape(HIDDEN, HIDDEN * cz)
     delta, lg, rg = pair_blocks(
-        row_size, col_size, left,
+        row_size, col_size, normed.reshape(rows * SEQS, CHANNELS), w_first,
         right.reshape(rows, HIDDEN * SEQS), w, bias.reshape(1, cz), cot)
     half = rows // col_size
     lg = lg.reshape(half * SEQS, HIDDEN)

time: 81 us -> 80.6 us (level)
  matrix products: 5.17 us -> 1.1 us
  other arithmetic: 3.51 us -> 7.39 us
  local copies, waits for them, and re-layouts: 17.3 us -> 15.9 us
  Pallas kernels: 51.6 us -> 52.8 us
    dot_general x1 -> x0, matrix products: 4.08 us -> none  [shards(): jnp.dot(normed.reshape(rows * SEQS, CHANNELS), w_first, preferred_element...]
    convert_element_type x1 -> x2, other arithmetic: 0.99 us -> 4.88 us  [shards(): normed = (standard * factor + shift).astype(jnp.bfloat16)]
    convert_element_type x1 -> x0, local copies, waits for them, and re-layouts: 2.08 us -> none  [shards(): left = jnp.dot(normed.reshape(rows * SEQS, CHANNELS), w_first, preferred_...]
    pallas_call x1, Pallas kernels: 51.6 us -> 52.8 us  [pair_blocks(): pl.pallas_call(functools.partial(pair_kernel, row_size, col_size), in_spe...]
    unnamed x26 -> x27, local copies, waits for them, and re-layouts: 5.7 us -> 6.39 us
where the time goes in v4:
time: 80.6 us; the launch traced here: 80.2 us
  Pallas kernels  52.8 us (66%)
  local copies, waits for them, and re-layouts  15.9 us (20%)
  other arithmetic  7.39 us (9%)
  blocking collectives  2.09 us (3%)
  matrix products  1.1 us (1%)
  between operations  0.91 us (1%)
    pallas_call x1, Pallas kernels, pair_blocks(): pl.pallas_call(functools.partial(pair_kernel, row_size, col_size), in_spe...  52.8 us
    unnamed x27, local copies, waits for them, and re-layouts  6.39 us
    convert_element_type x2, other arithmetic, shards(): normed = (standard * factor + shift).astype(jnp.bfloat16)  4.88 us
    all_gather x1, blocking collectives, shards(): grad = lax.all_gather(grad, 'col', axis=0, tiled=True)  2.09 us
    reshape x2, local copies, waits for them, and re-layouts, shards(): x = features.astype(jnp.float32).reshape(rows, SEQS, CHANNELS)  1.84 us
    reshape x3, local copies, waits for them, and re-layouts, shards(): rg.reshape(half, HIDDEN, SEQS).transpose(0, 2, 1)  1.73 us

profile of v4, /device:TPU:0, one launch (start us, length us, event | category | flops | bytes accessed | tf_op | source)
XLA Modules:
  0.0 80.2 jit_solution(9136090017061141394)
XLA Ops:
  0.6 1.4 %reshape.92 = f32[64,48,64]{2,1,0:T(8,128)S(1)} reshape(bf16[64,3072]{1,0:T(8,128)(2,1)} %param.8) | data formatting | bytes 1179648 | tf_op jit(solution)/shard_map/reshape | solution.py:298
  2.1 0.5 reduce_sum.36
  2.6 0.9 %multiply_reduce_fusion = f32[64,48]{1,0:T(8,128)S(1)} fusion(f32[64,48,64]{2,1,0:T(8,128)S(1)} %reshape.92, f32[64,48]{1,0:T(8,128)S(1)} %broadcast_multiply_fusion), kind=kLoop, calls=%fused_computation.2 | loop fusion | flops 586752 | bytes 811008 | tf_op jit(solution)/shard_map/reduce_sum | solution.py:300
  3.6 1.0 %add_convert_fusion = (bf16[64,48,64]{2,1,0:T(8,128)(2,1)S(1)}, f32[64,48,64]{2,1,0:T(8,128)S(1)}) fusion(f32[64]{0:T(128)S(1)} %copy-done.11, f32[64]{0:T(128)S(1)} %copy-done.9, f32[64,48]{1,0:T(8,128)S(1)} %add_rsqrt_fusion, f32[64,48,64]{2,1,0:T(8,128)S(1)} %reshape.92, f32[64,48]{1,0:T(8,128)S(1)} %broadcast_multiply_fusion), kind=kLoop, calls=%fused_computation | loop fusion | flops 983040 | bytes 1991168 | tf_op jit(solution)/shard_map/convert_element_type | solution.py:302
  4.6 0.8 %fusion = bf16[64,32,48]{0,1,2:T(8,128)(2,1)S(1)} fusion(bf16[64,48,64]{2,1,0:T(8,128)(2,1)S(1)} %get-tuple-element.8, bf16[64,32]{0,1:T(8,128)(2,1)S(1)} %copy-done.7), kind=kOutput, calls=%fused_computation.5 | convolution fusion | flops 12681216 | bytes 593920 | tf_op jit(solution)/shard_map/isc,ch->ihs/dot_general | solution.py:303
  5.5 1.0 %copy.21 = bf16[64,32,48]{2,1,0:T(8,128)(2,1)S(1)} copy(bf16[64,32,48]{0,1,2:T(8,128)(2,1)S(1)} %fusion) | data formatting | bytes 393216 | tf_op jit(solution)/shard_map/convert_element_type | solution.py:304
  6.4 1.5 %reshape.93.right_ref = bf16[64,1536]{1,0:T(8,128)(2,1)} reshape(bf16[64,32,48]{2,1,0:T(8,128)(2,1)S(1)} %copy.21) | data formatting | bytes 393216 | tf_op jit(solution)/shard_map/reshape | solution.py:309
  8.0 0.7 div.17
  8.7 0.4 reshape.91
  9.1 3.9 %add_convert_fusion.1.normed_ref = bf16[3072,64]{1,0:T(8,128)(2,1)} fusion(f32[3072,64]{1,0:T(8,128)S(1)} %reshape.91, f32[64]{0:T(128)} %param.10, f32[64]{0:T(128)S(1)} %copy-done.9, f32[3072]{0:T(1024)S(1)} %rsqrt.18, f32[3072]{0:T(1024)} %div.17), kind=kLoop, calls=%fused_computation.1 | loop fusion | flops 983040 | bytes 1204736 | tf_op jit(solution)/shard_map/convert_element_type | solution.py:302
  13.0 0.8 %reshape.94.w_ref = bf16[32,4096]{1,0:T(8,128)(2,1)} reshape(bf16[1024,128]{1,0:T(8,128)(2,1)S(1)} %copy-done.6) | data formatting | bytes 524288 | tf_op jit(solution)/shard_map/reshape | solution.py:306
  13.8 0.7 copy.22.first_ref
  14.5 52.8 %shard_map.95 = (bf16[64,256,128]{2,1,0:T(8,128)(2,1)}, f32[4,384,32]{2,1,0:T(8,128)}, f32[32,1536]{1,0:T(8,128)}) custom-call(bf16[3072,64]{1,0:T(8,128)(2,1)} %add_convert_fusion.1.normed_ref, bf16[64,32]{1,0:T(8,128)(2,1)} %copy.22.first_ref, bf16[64,1536]{1,0:T(8,128)(2,1)} %reshape.93.right_ref, bf16[32,4096]{1,0:T(8,128)(2,1)} %reshape.94.w_ref, ...), custom_call_target="tpu_custom_call" | custom-call | flops 20937965568 | bytes 8388608 | tf_op jit(solution)/shard_map/pallas_call | solution.py:254
  67.3 1.2 %reshape.97 = f32[32,32,48]{2,1,0:T(8,128)S(1)} reshape(f32[32,1536]{1,0:T(8,128)} %get-tuple-element.7) | data formatting | bytes 393216 | tf_op jit(solution)/shard_map/reshape | solution.py:312
  68.5 0.3 copy.30
  68.8 0.3 reshape.98
  69.1 1.4 %copy.24 = f32[1536,32]{0,1:T(8,128)S(1)} copy(f32[1536,32]{1,0:T(8,128)} %bitcast.18) | data formatting | bytes 393216 | tf_op jit(solution)/shard_map/reshape | solution.py:311
  70.8 0.3 copy.26
  71.1 0.3 multiply_reduce_fusion.1
  71.6 0.8 multiply_convert_fusion
  72.4 0.3 reshape.100
  72.7 2.1 %all_gather.3 = bf16[64,3072]{1,0:T(8,128)(2,1)S(1)} all-gather(bf16[32,3072]{1,0:T(8,128)(2,1)S(1)} %reshape.100), channel_id=1, replica_groups=mesh['group'=2,'row'=8,'col'=2] {'col'}, dimensions={0}, use_global_device_ids=true | all-gather | bytes 589824 | tf_op jit(solution)/shard_map/all_gather | solution.py:321
  74.8 4.7 %copy.33 = bf16[64,256,128]{2,1,0:T(8,128)(2,1)} copy(bf16[64,256,128]{2,1,0:T(8,128)(2,1)} %get-tuple-element.16) | data formatting | bytes 8388608
  79.5 0.7 copy.34
  (33 shorter events, 0.7 us)
Async XLA Ops:
  2.1 1.5 %copy-start.9 = (f32[64]{0:T(128)S(1)}, f32[64]{0:T(128)}, u32[]{:S(2)}) copy-start(f32[64]{0:T(128)} %param.9) | copy-start | bytes 772
  2.1 1.5 %copy-start.11 = (f32[64]{0:T(128)S(1)}, f32[64]{0:T(128)}, u32[]{:S(2)}) copy-start(f32[64]{0:T(128)} %param.10) | copy-start | bytes 772
  2.6 2.0 %copy-start.1 = (f32[64,48]{1,0:T(8,128)}, f32[64,48]{1,0:T(8,128)S(1)}, u32[]{:S(2)}) copy-start(f32[64,48]{1,0:T(8,128)S(1)} %broadcast_multiply_fusion) | copy-start | bytes 36868
  3.5 1.0 %copy-start.3 = (f32[64,48]{1,0:T(8,128)}, f32[64,48]{1,0:T(8,128)S(1)}, u32[]{:S(2)}) copy-start(f32[64,48]{1,0:T(8,128)S(1)} %add_rsqrt_fusion) | copy-start | bytes 36868
  3.6 1.0 %copy-start.7 = (bf16[64,32]{0,1:T(8,128)(2,1)S(1)}, bf16[64,32]{0,1:T(8,128)(2,1)}, u32[]{:S(2)}) copy-start(bf16[64,32]{0,1:T(8,128)(2,1)} %param.12) | copy-start | bytes 12292
  4.6 4.1 %copy-start = (bf16[64,3072]{1,0:T(8,128)(2,1)S(1)}, bf16[64,3072]{1,0:T(8,128)(2,1)}, u32[]{:S(2)}) copy-start(bf16[64,3072]{1,0:T(8,128)(2,1)} %param.8) | copy-start | bytes 1179652
  4.6 3.3 %copy-start.4 = (f32[64,48]{1,0:T(8,128)S(1)}, f32[64,48]{1,0:T(8,128)}, u32[]{:S(2)}) copy-start(f32[64,48]{1,0:T(8,128)} %copy-done.3) | copy-start | bytes 36868
  4.6 3.4 %copy-start.2 = (f32[64,48]{1,0:T(8,128)S(1)}, f32[64,48]{1,0:T(8,128)}, u32[]{:S(2)}) copy-start(f32[64,48]{1,0:T(8,128)} %copy-done.1) | copy-start | bytes 36868
  9.1 3.9 %copy-start.6 = (bf16[1024,128]{1,0:T(8,128)(2,1)S(1)}, bf16[1024,128]{1,0:T(8,128)(2,1)}, u32[]{:S(2)}) copy-start(bf16[1024,128]{1,0:T(8,128)(2,1)} %param.13) | copy-start | bytes 786436
  9.1 4.7 %copy-start.10 = (bf16[64,32]{0,1:T(8,128)(2,1)S(1)}, bf16[64,32]{0,1:T(8,128)(2,1)}, u32[]{:S(2)}) copy-start(bf16[64,32]{0,1:T(8,128)(2,1)} %param.11) | copy-start | bytes 12292
  68.8 1.7 %copy-start.8 = (bf16[64,32]{0,1:T(8,128)(2,1)S(1)}, bf16[64,32]{0,1:T(8,128)(2,1)}, u32[]{:S(2)}) copy-start(bf16[64,32]{0,1:T(8,128)(2,1)} %param.12) | copy-start | bytes 12292
  70.8 0.8 copy-start.5

commit v5 on v4

--- a/solution.py
+++ b/solution.py
@@ -300,6 +300,7 @@
     inverse = lax.rsqrt(jnp.mean(center * center, axis=-1, keepdims=True) + 1e-05)
     standard = center * inverse
     normed = (standard * factor + shift).astype(jnp.bfloat16)
+    normed, standard, inverse = lax.optimization_barrier((normed, standard, inverse))
     right = jnp.einsum("isc,ch->ihs", normed, w_second,
                        preferred_element_type=jnp.float32).astype(jnp.bfloat16)
     cz = w_out.shape[1]

time: 80.6 us -> 76 us (0.943)
  other arithmetic: 7.39 us -> 3.53 us
    convert_element_type x2 -> x1, other arithmetic: 4.88 us -> 0.99 us  [shards(): normed = (standard * factor + shift).astype(jnp.bfloat16)]
    unnamed x27 -> x15, local copies, waits for them, and re-layouts: 6.39 us -> 7.02 us
    reshape x2 -> x1, local copies, waits for them, and re-layouts: 1.84 us -> 1.42 us  [shards(): x = features.astype(jnp.float32).reshape(rows, SEQS, CHANNELS)]
where the time goes in v5:
time: 76 us; the launch traced here: 75.7 us
  Pallas kernels  52.8 us (69%)
  local copies, waits for them, and re-layouts  15.4 us (20%)
  other arithmetic  3.53 us (5%)
  blocking collectives  2.09 us (3%)
  matrix products  1.1 us (1%)
  between operations  0.83 us (1%)
    pallas_call x1, Pallas kernels, pair_blocks(): pl.pallas_call(functools.partial(pair_kernel, row_size, col_size), in_spe...  52.8 us
    unnamed x15, local copies, waits for them, and re-layouts  7.02 us
    all_gather x1, blocking collectives, shards(): grad = lax.all_gather(grad, 'col', axis=0, tiled=True)  2.09 us
    reshape x3, local copies, waits for them, and re-layouts, shards(): rg.reshape(half, HIDDEN, SEQS).transpose(0, 2, 1)  1.73 us

profile of v5, /device:TPU:0, one launch (start us, length us, event | category | flops | bytes accessed | tf_op | source)
XLA Modules:
  0.0 75.7 jit_solution(11933015244630915904)
XLA Ops:
  0.6 1.4 %reshape.90 = f32[64,48,64]{2,1,0:T(8,128)S(1)} reshape(bf16[64,3072]{1,0:T(8,128)(2,1)} %param.8) | data formatting | bytes 1179648 | tf_op jit(solution)/shard_map/reshape | solution.py:298
  2.1 0.5 reduce_sum.36
  2.6 0.9 %multiply_reduce_fusion = f32[64,48]{1,0:T(8,128)S(1)} fusion(f32[64,48,64]{2,1,0:T(8,128)S(1)} %reshape.90, f32[64,48]{1,0:T(8,128)S(1)} %broadcast_multiply_fusion), kind=kLoop, calls=%fused_computation.1 | loop fusion | flops 586752 | bytes 811008 | tf_op jit(solution)/shard_map/reduce_sum | solution.py:300
  3.5 1.0 %add_convert_fusion = (bf16[64,48,64]{2,1,0:T(8,128)(2,1)S(1)}, f32[64,48,64]{2,1,0:T(8,128)S(1)}) fusion(f32[64]{0:T(128)S(1)} %copy-done.5, f32[64]{0:T(128)S(1)} %copy-done.4, f32[64,48]{1,0:T(8,128)S(1)} %get-tuple-element.17, f32[64,48,64]{2,1,0:T(8,128)S(1)} %reshape.90, f32[64,48]{1,0:T(8,128)S(1)} %broadcast_multiply_fusion), kind=kLoop, calls=%fused_computation | loop fusion | flops 983040 | bytes 1991168 | tf_op jit(solution)/shard_map/convert_element_type | solution.py:302
  4.6 0.9 %copy-done = bf16[64,48,64]{2,1,0:T(8,128)(2,1)} copy-done((bf16[64,48,64]{2,1,0:T(8,128)(2,1)}, bf16[64,48,64]{2,1,0:T(8,128)(2,1)S(1)}, u32[]{:S(2)}) %copy-start) | copy-done | bytes 393240
  5.4 0.8 %fusion = bf16[64,32,48]{0,1,2:T(8,128)(2,1)S(1)} fusion(bf16[64,48,64]{2,1,0:T(8,128)(2,1)S(1)} %get-tuple-element.8, bf16[64,32]{0,1:T(8,128)(2,1)S(1)} %copy-done.2), kind=kOutput, calls=%fused_computation.4 | convolution fusion | flops 12681216 | bytes 593920 | tf_op jit(solution)/shard_map/isc,ch->ihs/dot_general | solution.py:304
  6.3 1.0 %copy.23 = bf16[64,32,48]{2,1,0:T(8,128)(2,1)S(1)} copy(bf16[64,32,48]{0,1,2:T(8,128)(2,1)S(1)} %fusion) | data formatting | bytes 393216 | tf_op jit(solution)/shard_map/convert_element_type | solution.py:305
  7.2 1.5 %reshape.81.right_ref = bf16[64,1536]{1,0:T(8,128)(2,1)} reshape(bf16[64,32,48]{2,1,0:T(8,128)(2,1)S(1)} %copy.23) | data formatting | bytes 393216 | tf_op jit(solution)/shard_map/reshape | solution.py:310
  8.7 0.8 %reshape.82.w_ref = bf16[32,4096]{1,0:T(8,128)(2,1)} reshape(bf16[1024,128]{1,0:T(8,128)(2,1)S(1)} %copy-done.1) | data formatting | bytes 524288 | tf_op jit(solution)/shard_map/reshape | solution.py:307
  9.5 0.7 copy.24.first_ref
  10.2 52.8 %shard_map.95 = (bf16[64,256,128]{2,1,0:T(8,128)(2,1)}, f32[4,384,32]{2,1,0:T(8,128)}, f32[32,1536]{1,0:T(8,128)}) custom-call(bf16[3072,64]{1,0:T(8,128)(2,1)} %bitcast.22, bf16[64,32]{1,0:T(8,128)(2,1)} %copy.24.first_ref, bf16[64,1536]{1,0:T(8,128)(2,1)} %reshape.81.right_ref, bf16[32,4096]{1,0:T(8,128)(2,1)} %reshape.82.w_ref, f32[1,128]{1,0:T(1,128)} %bitcast.27, ...), custom_call_target="tpu_custom_call" | custom-call | flops 20937965568 | bytes 8388608 | tf_op jit(solution)/shard_map/pallas_call | solution.py:254
  63.0 1.2 %reshape.85 = f32[32,32,48]{2,1,0:T(8,128)S(1)} reshape(f32[32,1536]{1,0:T(8,128)} %get-tuple-element.12) | data formatting | bytes 393216 | tf_op jit(solution)/shard_map/reshape | solution.py:313
  64.2 0.3 copy.32
  64.5 0.3 reshape.86
  64.8 1.4 %copy.26 = f32[1536,32]{0,1:T(8,128)S(1)} copy(f32[1536,32]{1,0:T(8,128)} %bitcast.24) | data formatting | bytes 393216 | tf_op jit(solution)/shard_map/reshape | solution.py:312
  66.2 0.3 multiply_reduce_fusion.2
  66.5 0.3 copy.28
  66.7 0.3 multiply_reduce_fusion.1
  67.0 0.1 div.17
  67.1 0.8 %multiply_convert_fusion = bf16[32,48,64]{2,1,0:T(8,128)(2,1)S(1)} fusion(f32[32,48,64]{2,1,0:T(8,128)S(1)} %bitcast.21, f32[64,48,64]{2,1,0:T(8,128)S(1)} %get-tuple-element.13, s32[]{:T(128)S(6)} %select_n.4, f32[32,48]{1,0:T(8,128)S(1)} %broadcast_multiply_fusion.1, f32[32,48]{1,0:T(8,128)S(1)} %div.17, f32[64]{0:T(128)S(1)} %copy-done.4, ...), kind=kLoop, calls=%fused_computation.6 | loop fusion | flops 589824 | bytes 1001732 | tf_op jit(solution)/shard_map/convert_element_type | solution.py:321
  67.9 0.3 reshape.88
  68.2 2.1 %all_gather.3 = bf16[64,3072]{1,0:T(8,128)(2,1)S(1)} all-gather(bf16[32,3072]{1,0:T(8,128)(2,1)S(1)} %reshape.88), channel_id=1, replica_groups=mesh['group'=2,'row'=8,'col'=2] {'col'}, dimensions={0}, use_global_device_ids=true | all-gather | bytes 589824 | tf_op jit(solution)/shard_map/all_gather | solution.py:322
  70.3 4.7 %copy.35 = bf16[64,256,128]{2,1,0:T(8,128)(2,1)} copy(bf16[64,256,128]{2,1,0:T(8,128)(2,1)} %get-tuple-element.22) | data formatting | bytes 8388608
  75.0 0.7 copy.36
  (18 shorter events, 0.1 us)
Async XLA Ops:
  2.1 1.5 %copy-start.4 = (f32[64]{0:T(128)S(1)}, f32[64]{0:T(128)}, u32[]{:S(2)}) copy-start(f32[64]{0:T(128)} %param.9) | copy-start | bytes 772
  2.1 1.5 %copy-start.5 = (f32[64]{0:T(128)S(1)}, f32[64]{0:T(128)}, u32[]{:S(2)}) copy-start(f32[64]{0:T(128)} %param.10) | copy-start | bytes 772
  3.5 1.9 %copy-start.2 = (bf16[64,32]{0,1:T(8,128)(2,1)S(1)}, bf16[64,32]{0,1:T(8,128)(2,1)}, u32[]{:S(2)}) copy-start(bf16[64,32]{0,1:T(8,128)(2,1)} %param.12) | copy-start | bytes 12292
  4.5 0.9 %copy-start = (bf16[64,48,64]{2,1,0:T(8,128)(2,1)}, bf16[64,48,64]{2,1,0:T(8,128)(2,1)S(1)}, u32[]{:S(2)}) copy-start(bf16[64,48,64]{2,1,0:T(8,128)(2,1)S(1)} %get-tuple-element.8) | copy-start | bytes 1179652
  4.6 4.2 %copy-start.1 = (bf16[1024,128]{1,0:T(8,128)(2,1)S(1)}, bf16[1024,128]{1,0:T(8,128)(2,1)}, u32[]{:S(2)}) copy-start(bf16[1024,128]{1,0:T(8,128)(2,1)} %param.13) | copy-start | bytes 786436
  5.4 4.1 %copy-start.3 = (bf16[64,32]{0,1:T(8,128)(2,1)S(1)}, bf16[64,32]{0,1:T(8,128)(2,1)}, u32[]{:S(2)}) copy-start(bf16[64,32]{0,1:T(8,128)(2,1)} %param.11) | copy-start | bytes 12292

commit v6 on v5

--- a/solution.py
+++ b/solution.py
@@ -311,8 +311,7 @@
     half = rows // col_size
     lg = lg.reshape(half * SEQS, HIDDEN)
     rg = rg.reshape(half, HIDDEN, SEQS).transpose(0, 2, 1).reshape(half * SEQS, HIDDEN)
-    d = split_dot(jnp.concatenate([lg, rg], axis=-1),
-                  jnp.concatenate([w_first.T, w_second.T], axis=0))
+    d = split_dot(lg, w_first.T) + split_dot(rg, w_second.T)
     e = d.reshape(half, SEQS, CHANNELS) * factor
     std = lax.dynamic_slice_in_dim(standard, col * half, half, 0)
     inv = lax.dynamic_slice_in_dim(inverse, col * half, half, 0)

time: 76 us -> 76 us (level)
  local copies, waits for them, and re-layouts: 15.4 us -> 13.2 us
  other arithmetic: 3.53 us -> 5.34 us
    reshape x1 -> x0, local copies, waits for them, and re-layouts: 1.37 us -> none  [shards(): lg = lg.reshape(half * SEQS, HIDDEN)]
    convert_element_type x1 -> x2, other arithmetic: 0.03 us -> 1.29 us  [split_dot(): low = (x - high.astype(jnp.float32)).astype(jnp.bfloat16)]
    reshape x3, local copies, waits for them, and re-layouts: 1.73 us -> 0.8 us  [shards(): rg.reshape(half, HIDDEN, SEQS).transpose(0, 2, 1)]
    unnamed x15 -> x19, local copies, waits for them, and re-layouts: 7.02 us -> 7.12 us
where the time goes in v6:
time: 76 us; the launch traced here: 75.7 us
  Pallas kernels  52.8 us (69%)
  local copies, waits for them, and re-layouts  13.2 us (17%)
  other arithmetic  5.34 us (7%)
  blocking collectives  2.09 us (3%)
  matrix products  1.48 us (2%)
  between operations  0.82 us (1%)
    pallas_call x1, Pallas kernels, pair_blocks(): pl.pallas_call(functools.partial(pair_kernel, row_size, col_size), in_spe...  52.8 us
    unnamed x19, local copies, waits for them, and re-layouts  7.12 us
    all_gather x1, blocking collectives, shards(): grad = lax.all_gather(grad, 'col', axis=0, tiled=True)  2.09 us

profile of v6, /device:TPU:0, one launch (start us, length us, event | category | flops | bytes accessed | tf_op | source)
XLA Modules:
  0.0 75.7 jit_solution(10505280986552005538)
XLA Ops:
  0.6 1.4 %reshape.90 = f32[64,48,64]{2,1,0:T(8,128)S(1)} reshape(bf16[64,3072]{1,0:T(8,128)(2,1)} %param.8) | data formatting | bytes 1179648 | tf_op jit(solution)/shard_map/reshape | solution.py:298
  2.1 0.5 reduce_sum.36
  2.6 0.9 %multiply_reduce_fusion = f32[64,48]{1,0:T(8,128)S(1)} fusion(f32[64,48,64]{2,1,0:T(8,128)S(1)} %reshape.90, f32[64,48]{1,0:T(8,128)S(1)} %broadcast_multiply_fusion), kind=kLoop, calls=%fused_computation.2 | loop fusion | flops 586752 | bytes 811008 | tf_op jit(solution)/shard_map/reduce_sum | solution.py:300
  3.5 0.6 fusion.19
  4.1 1.0 %add_convert_fusion = (bf16[64,48,64]{2,1,0:T(8,128)(2,1)S(1)}, f32[64,48,64]{2,1,0:T(8,128)S(1)}) fusion(f32[64]{0:T(128)S(1)} %copy-done.7, f32[64]{0:T(128)S(1)} %copy-done.6, f32[64,48]{1,0:T(8,128)S(1)} %get-tuple-element.21, f32[64,48,64]{2,1,0:T(8,128)S(1)} %reshape.90, f32[64,48]{1,0:T(8,128)S(1)} %broadcast_multiply_fusion), kind=kLoop, calls=%fused_computation.1 | loop fusion | flops 983040 | bytes 1991168 | tf_op jit(solution)/shard_map/convert_element_type | solution.py:302
  5.1 0.9 %copy-done = bf16[64,48,64]{2,1,0:T(8,128)(2,1)} copy-done((bf16[64,48,64]{2,1,0:T(8,128)(2,1)}, bf16[64,48,64]{2,1,0:T(8,128)(2,1)S(1)}, u32[]{:S(2)}) %copy-start) | copy-done | bytes 393240
  6.0 0.8 %fusion = bf16[64,32,48]{0,1,2:T(8,128)(2,1)S(1)} fusion(bf16[64,48,64]{2,1,0:T(8,128)(2,1)S(1)} %get-tuple-element.8, bf16[64,32]{0,1:T(8,128)(2,1)S(1)} %copy-done.4), kind=kOutput, calls=%fused_computation.5 | convolution fusion | flops 12681216 | bytes 593920 | tf_op jit(solution)/shard_map/isc,ch->ihs/dot_general | solution.py:304
  6.8 1.0 %copy.22 = bf16[64,32,48]{2,1,0:T(8,128)(2,1)S(1)} copy(bf16[64,32,48]{0,1,2:T(8,128)(2,1)S(1)} %fusion) | data formatting | bytes 393216 | tf_op jit(solution)/shard_map/convert_element_type | solution.py:305
  7.8 1.5 %reshape.81.right_ref = bf16[64,1536]{1,0:T(8,128)(2,1)} reshape(bf16[64,32,48]{2,1,0:T(8,128)(2,1)S(1)} %copy.22) | data formatting | bytes 393216 | tf_op jit(solution)/shard_map/reshape | solution.py:310
  9.3 0.8 %reshape.82.w_ref = bf16[32,4096]{1,0:T(8,128)(2,1)} reshape(bf16[1024,128]{1,0:T(8,128)(2,1)S(1)} %copy-done.1) | data formatting | bytes 524288 | tf_op jit(solution)/shard_map/reshape | solution.py:307
  10.1 0.7 copy.23.first_ref
  10.8 52.8 %shard_map.95 = (bf16[64,256,128]{2,1,0:T(8,128)(2,1)}, f32[4,384,32]{2,1,0:T(8,128)}, f32[32,1536]{1,0:T(8,128)}) custom-call(bf16[3072,64]{1,0:T(8,128)(2,1)} %bitcast.27, bf16[64,32]{1,0:T(8,128)(2,1)} %copy.23.first_ref, bf16[64,1536]{1,0:T(8,128)(2,1)} %reshape.81.right_ref, bf16[32,4096]{1,0:T(8,128)(2,1)} %reshape.82.w_ref, f32[1,128]{1,0:T(1,128)} %bitcast.31, ...), custom_call_target="tpu_custom_call" | custom-call | flops 20937965568 | bytes 8388608 | tf_op jit(solution)/shard_map/pallas_call | solution.py:254
  63.6 1.3 %fusion.1 = (bf16[1536,32]{1,0:T(8,128)(2,1)S(1)}, bf16[1536,32]{1,0:T(8,128)(2,1)S(1)}) fusion(f32[4,384,32]{2,1,0:T(8,128)} %get-tuple-element.11), kind=kLoop, calls=%fused_computation.8 | loop fusion | flops 196608 | bytes 393216 | tf_op jit(solution)/shard_map/convert_element_type | solution.py:288
  64.9 0.4 fusion.3
  65.5 0.3 copy.30
  65.8 0.3 reshape.86
  66.1 0.3 multiply_reduce_fusion.2
  66.4 0.3 copy.26
  66.7 0.3 multiply_reduce_fusion.1
  67.1 0.8 %multiply_convert_fusion = bf16[32,48,64]{2,1,0:T(8,128)(2,1)S(1)} fusion(f32[32,48,64]{2,1,0:T(8,128)S(1)} %bitcast.26, f32[64,48,64]{2,1,0:T(8,128)S(1)} %get-tuple-element.13, s32[]{:T(128)S(6)} %select_n.4, f32[32,48]{1,0:T(8,128)S(1)} %broadcast_multiply_fusion.1, f32[32,48]{1,0:T(8,128)S(1)} %div.17, f32[64]{0:T(128)S(1)} %copy-done.6, ...), kind=kLoop, calls=%fused_computation.10 | loop fusion | flops 589824 | bytes 1001732 | tf_op jit(solution)/shard_map/convert_element_type | solution.py:320
  67.9 0.3 reshape.88
  68.2 2.1 %all_gather.3 = bf16[64,3072]{1,0:T(8,128)(2,1)S(1)} all-gather(bf16[32,3072]{1,0:T(8,128)(2,1)S(1)} %reshape.88), channel_id=1, replica_groups=mesh['group'=2,'row'=8,'col'=2] {'col'}, dimensions={0}, use_global_device_ids=true | all-gather | bytes 589824 | tf_op jit(solution)/shard_map/all_gather | solution.py:321
  70.3 4.7 %copy.33 = bf16[64,256,128]{2,1,0:T(8,128)(2,1)} copy(bf16[64,256,128]{2,1,0:T(8,128)(2,1)} %get-tuple-element.26) | data formatting | bytes 8388608
  75.0 0.7 copy.34
  (22 shorter events, 0.5 us)
Async XLA Ops:
  2.1 2.1 %copy-start.6 = (f32[64]{0:T(128)S(1)}, f32[64]{0:T(128)}, u32[]{:S(2)}) copy-start(f32[64]{0:T(128)} %param.9) | copy-start | bytes 772
  2.1 2.1 %copy-start.7 = (f32[64]{0:T(128)S(1)}, f32[64]{0:T(128)}, u32[]{:S(2)}) copy-start(f32[64]{0:T(128)} %param.10) | copy-start | bytes 772
  4.1 1.9 %copy-start.4 = (bf16[64,32]{0,1:T(8,128)(2,1)S(1)}, bf16[64,32]{0,1:T(8,128)(2,1)}, u32[]{:S(2)}) copy-start(bf16[64,32]{0,1:T(8,128)(2,1)} %param.12) | copy-start | bytes 12292
  5.1 0.9 %copy-start = (bf16[64,48,64]{2,1,0:T(8,128)(2,1)}, bf16[64,48,64]{2,1,0:T(8,128)(2,1)S(1)}, u32[]{:S(2)}) copy-start(bf16[64,48,64]{2,1,0:T(8,128)(2,1)S(1)} %get-tuple-element.8) | copy-start | bytes 1179652
  5.1 4.2 %copy-start.1 = (bf16[1024,128]{1,0:T(8,128)(2,1)S(1)}, bf16[1024,128]{1,0:T(8,128)(2,1)}, u32[]{:S(2)}) copy-start(bf16[1024,128]{1,0:T(8,128)(2,1)} %param.13) | copy-start | bytes 786436
  6.0 4.1 %copy-start.5 = (bf16[64,32]{0,1:T(8,128)(2,1)S(1)}, bf16[64,32]{0,1:T(8,128)(2,1)}, u32[]{:S(2)}) copy-start(bf16[64,32]{0,1:T(8,128)(2,1)} %param.11) | copy-start | bytes 12292
  63.6 1.7 %copy-start.2 = (f32[32,1536]{1,0:T(8,128)S(1)}, f32[32,1536]{1,0:T(8,128)}, u32[]{:S(2)}) copy-start(f32[32,1536]{1,0:T(8,128)} %get-tuple-element.12) | copy-start | bytes 589828
  66.4 0.8 %copy-start.3 = (f32[64,48,1]{1,0,2:T(8,128)S(1)}, f32[64,48,1]{1,0,2:T(8,128)}, u32[]{:S(2)}) copy-start(f32[64,48,1]{1,0,2:T(8,128)} %get-tuple-element.10) | copy-start | bytes 36868
